TPU v7x, 256 devices: a whole 4x4x8 slice. The times are simulated.
256 devices in a mesh: cent: 16 (over y, x), pass: 16 (over z, core).
Axes of the slice: x: 4, y: 4, z: 8, core: 2. Of those that a mesh axis runs over, the one named last changes fastest.
Arguments:
- queries: bfloat16 [1024, 32, 128], P(('cent', 'pass')), may hold values from -6 to 6
- probes: int32 [1024, 4], replicated, may hold values from 0 to 262143
- centroids: bfloat16 [262144, 128], P('cent'), may hold values from -0.5 to 0.5
- codebook: float32 [4, 128], replicated, may hold values from -0.9 to 0.9
- token_cells: int32 [384, 30], P('pass'), may hold values from 0 to 262143
- codes: int32 [384, 2, 128], P('pass'), may hold values from 0 to 1073741823
- locations: int32 [384], replicated, may hold values from 0 to 383, as said below
- candidates: int32 [1024, 40], P(('cent', 'pass')), may hold values from 0 to 383, as said below
- lengths: int32 [1024], P(('cent', 'pass')), may hold values from 3 to 33
Outputs:
- top_scores: float32 [1024, 32], P(('cent', 'pass'))
- probe_scores: float32 [1024, 32, 4], P(('cent', 'pass'))
- maxsim: float32 [1024, 40], P(('cent', 'pass'))
Inputs may be any that keep to these rules, and one draw needn't show every extreme that they name: A permutation: passage id i is stored by passage owner locations[i] // 24 at its slot locations[i] % 24. `candidates`: the first lengths[q] slots of query q hold distinct passage ids; at most 3 of them are stored by one passage owner, and for every query some owner stores exactly 3; later slots hold any passage ids.
All inputs are finite; a program needn't handle non-finite values.
Results may differ from a plain program's by a relative error of at most 0.00055.
Values may be sent and summed in bfloat16 or wider, within the bound.
A program may use at most 64 MiB of HBM per device.

v0:
```python
import math

import jax
import jax.numpy as jnp
from jax import lax
from jax.sharding import PartitionSpec as P

DIM = 128
QT = 32
NPROBE = 4
CAP = 3
CMAX = 40


def unpack_levels(codes):
    n_rows, n_groups, n_width = codes.shape
    shifts = 2 * jnp.arange(15, dtype=jnp.int32)
    levels = jnp.bitwise_and(jnp.right_shift(codes[:, :, None, :], shifts[None, None, :, None]), 3)
    return levels.reshape(n_rows, n_groups * 15, n_width)


def decode_rows(cell_rows, levels, codebook):
    one_hot = (levels[..., None] == jnp.arange(4, dtype=jnp.int32)).astype(jnp.float32)
    residual = jnp.sum(one_hot * jnp.transpose(codebook)[None, None, :, :], axis=-1)
    vector = cell_rows + residual
    squares = jnp.sum(vector * vector, axis=-1, keepdims=True)
    return (vector * lax.rsqrt(squares + 1e-06)).astype(jnp.bfloat16)


def body(queries, probes, centroids, codebook, token_cells, codes, locations, candidates, lengths):
    n_cent = lax.axis_size("cent")
    n_pass = lax.axis_size("pass")
    cent_pos = lax.axis_index("cent")
    pass_pos = lax.axis_index("pass")
    q_dev = queries.shape[0]
    cent_dev = centroids.shape[0]
    own_count = codes.shape[0]
    passage_len = token_cells.shape[1]
    npass_all = locations.shape[0]
    grouped = lax.all_gather(queries, "cent", axis=0, tiled=True)
    flattened = grouped.reshape(n_cent * q_dev * QT, DIM)
    block_size = math.gcd(cent_dev, 2048)

    def scan_block(running, offset):
        block_rows = lax.dynamic_slice_in_dim(centroids, offset, block_size, 0)
        partial_value = lax.dot_general(
            flattened, block_rows, (((1,), (1,)), ((), ())), preferred_element_type=jnp.float32
        )
        return (jnp.maximum(running, jnp.max(partial_value, axis=1)), None)

    starts = jnp.arange(cent_dev // block_size, dtype=jnp.int32) * block_size
    running, unused = lax.scan(
        scan_block, jnp.full((flattened.shape[0],), -1e30, jnp.float32), starts
    )
    group_probes = lax.dynamic_index_in_dim(
        probes.reshape(n_cent, n_pass, q_dev * NPROBE), pass_pos, 1, keepdims=False
    ).reshape(n_cent * q_dev, NPROBE)
    local_ids = group_probes - cent_pos * cent_dev
    inside = (local_ids >= 0) & (local_ids < cent_dev)
    probe_rows = jnp.take(centroids, jnp.clip(local_ids, 0, cent_dev - 1), axis=0)
    probe_terms = jnp.einsum(
        "gtd,gpd->gtp", grouped, probe_rows, preferred_element_type=jnp.float32
    )
    inside_mask = inside[:, None, :]
    cell_ids = token_cells - cent_pos * cent_dev
    cell_inside = (cell_ids >= 0) & (cell_ids < cent_dev)
    cell_rows = jnp.take(centroids, jnp.clip(cell_ids, 0, cent_dev - 1), axis=0)
    cell_terms = jnp.where(cell_inside[..., None], cell_rows.astype(jnp.float32), 0.0)
    cell_sum = lax.psum(cell_terms.astype(jnp.bfloat16), "cent").astype(jnp.float32)
    best_all = lax.pmax(running, "cent")
    probe_all = lax.psum(jnp.where(inside_mask, probe_terms, 0.0), "cent")
    top_scores = lax.dynamic_index_in_dim(
        best_all.reshape(n_cent, q_dev, QT), cent_pos, 0, keepdims=False
    )
    probe_scores = lax.dynamic_index_in_dim(
        probe_all.reshape(n_cent, q_dev, QT, NPROBE), cent_pos, 0, keepdims=False
    )
    stored = decode_rows(cell_sum, unpack_levels(codes), codebook)
    store_flat = stored.reshape(own_count, passage_len * DIM)
    match_table = candidates[..., None] == jnp.arange(npass_all, dtype=jnp.int32)
    positions = jnp.sum(jnp.where(match_table, locations[None, None, :], 0), axis=-1)
    live_slots = jnp.arange(CMAX, dtype=jnp.int32)[None, :] < lengths[:, None]
    owners = positions // own_count
    storage_slot = positions % own_count
    owner_hit = (owners[..., None] == jnp.arange(n_pass, dtype=jnp.int32)) & live_slots[..., None]
    hit_count = owner_hit.astype(jnp.int32)
    before = jnp.cumsum(hit_count, axis=1) - hit_count
    owner_rank = jnp.sum(before * hit_count, axis=2)
    placement = owner_hit[..., None] & (
        owner_rank[:, :, None, None] == jnp.arange(CAP, dtype=jnp.int32)
    )
    requests = jnp.transpose(
        jnp.sum(jnp.where(placement, storage_slot[:, :, None, None], 0), axis=1), (1, 0, 2)
    )
    blocks = jnp.take(
        store_flat,
        lax.all_to_all(requests, "pass", split_axis=0, concat_axis=0, tiled=True),
        axis=0,
    )
    arrived = lax.all_to_all(blocks, "pass", split_axis=0, concat_axis=0, tiled=True)
    bucket_width = arrived.shape[2]
    tokens = arrived.reshape(n_pass, q_dev, bucket_width * passage_len, DIM)
    similarity = jnp.einsum("qtd,oqbd->qtob", queries, tokens, preferred_element_type=jnp.float32)
    per_slot = jnp.mean(
        jnp.max(similarity.reshape(q_dev, QT, n_pass, bucket_width, passage_len), axis=4), axis=1
    )
    bucket = jnp.transpose(per_slot, (1, 0, 2))
    by_query = jnp.transpose(bucket, (1, 0, 2))
    mean_scores = jnp.sum(jnp.where(placement, by_query[:, None, :, :], 0.0), axis=(2, 3))
    maxsim = jnp.where(live_slots, mean_scores, 0.0)
    return (top_scores, probe_scores, maxsim)


def solution(mesh):
    placed = (
        P(("cent", "pass"), None, None),
        P(),
        P("cent", None),
        P(),
        P("pass", None),
        P("pass", None, None),
        P(),
        P(("cent", "pass"), None),
        P(("cent", "pass")),
    )
    return jax.shard_map(
        body,
        mesh=mesh,
        in_specs=placed,
        out_specs=(
            P(("cent", "pass"), None),
            P(("cent", "pass"), None, None),
            P(("cent", "pass"), None),
        ),
        check_vma=False,
    )
```

profile of v0, /device:TPU:32, one launch (start us, length us, event | category | flops | bytes accessed | tf_op | source)
XLA Modules:
  0.0 337.3 jit_solution(811169301501558028)
XLA Ops:
  7.3 0.7 compare_and_fusion.2
  8.1 4.5 %gather_fusion.1 = bf16[720,128]{1,0:T(8,128)(2,1)S(1)} fusion(bf16[16384,128]{1,0:T(8,128)(2,1)} %param.13, s32[1024]{0:T(1024)S(1)} %pad_clamp_fusion.1), kind=kCustom, calls=%fused_computation.1 | custom fusion | bytes 371520 | tf_op jit(solution)/shard_map/jit(_take)/gather | solution.py:67
  12.9 0.9 select_convert_fusion
  14.4 0.2 select_reduce_fusion.2
  14.8 0.3 fusion.4
  15.1 0.7 copy.43
  15.8 8.6 %all-to-all-start = ((s32[16,4,3]{2,1,0:T(4,128)}), s32[16,4,3]{2,1,0:T(4,128)S(1)}, u32[]{:S(2)}, u32[]{:S(2)}) async-start(s32[16,4,3]{2,1,0:T(4,128)} %copy.43), calls=%async_computation | async-start | bytes 65536 | tf_op jit(solution)/shard_map/all_to_all | solution.py:97
  24.9 0.5 broadcast.234
  25.4 0.7 fusion.14
  26.3 4.1 %gather_fusion = bf16[256,128]{1,0:T(8,128)(2,1)} fusion(bf16[16384,128]{1,0:T(8,128)(2,1)} %param.13, s32[1024]{0:T(1024)S(1)} %pad_clamp_fusion.2), kind=kCustom, calls=%fused_computation | custom fusion | bytes 132096 | tf_op jit(solution)/shard_map/jit(_take)/gather | solution.py:60
  30.5 26.3 %all_gather.3 = bf16[64,32,128]{2,1,0:T(8,128)(2,1)} all-gather(bf16[4,32,128]{2,1,0:T(8,128)(2,1)S(1)} %copy-done.1), channel_id=1, replica_groups=mesh['cent'=16,'pass'=16] {'cent'}, dimensions={0}, use_global_device_ids=true | all-gather | bytes 557056 | tf_op jit(solution)/shard_map/all_gather | solution.py:40
  57.5 52.8 %all-reduce.2.cloned.1.call-done = bf16[24,30,128]{2,0,1:T(8,128)(2,1)} async-done(((bf16[24,30,128]{2,0,1:T(8,128)(2,1)}), bf16[24,30,128]{2,0,1:T(8,128)(2,1)}) %all-reduce.2.cloned.1.call-update) | async-done | bytes 184336 | tf_op jit(solution)/shard_map/psum | solution.py:69
  110.2 1.1 multiply_reduce_fusion
  111.3 1.1 copy_bitcast_fusion
  112.4 1.5 gather_fusion.2
  113.9 0.7 reshape.191
  114.6 1.0 broadcast_select_fusion
  115.6 1.8 copy.49
  117.4 7.6 %all-to-all-start.1 = ((bf16[16,4,3,3840]{3,1,2,0:T(4,128)(2,1)}), bf16[16,4,3,3840]{3,1,2,0:T(4,128)(2,1)S(1)}, u32[]{:S(2)}, u32[]{:S(2)}) async-start(bf16[16,4,3,3840]{3,1,2,0:T(4,128)(2,1)} %copy.49), calls=%async_computation.1 | async-start | bytes 2949120 | tf_op jit(solution)/shard_map/all_to_all | solution.py:100
  125.0 47.8 %while.11 = (s32[]{:T(128)}, f32[2048]{0:T(1024)S(1)}, s32[8]{0:T(128)S(1)}, bf16[16384,128]{1,0:T(8,128)(2,1)}, bf16[2048,128]{1,0:T(8,128)(2,1)S(1)}, /*index=5*/s32[]{:T(128)}, s32[]{:T(128)}, s32[]{:T(128)}) while((s32[]{:T(128)}, f32[2048]{0:T(1024)S(1)}, s32[8]{0:T(128)S(1)}, bf16[16384,128]{1,0:T(8,128)(2,1)}, ...), condition=%wide.region_2.3_spmd.clone, body=%wide.region_0.2_spmd.clone.sunk | while | flops 1077938176 | bytes 1081489 | solution.py:52
  125.1 0.6 dynamic_slice.37
  127.6 3.4 %convolution_reduce_fusion.2 = f32[2048]{0:T(1024)S(1)} fusion(bf16[2048,128]{1,0:T(8,128)(2,1)S(1)} %get-tuple-element.119, bf16[16384,128]{1,0:T(8,128)(2,1)} %get-tuple-element.118, s32[]{:T(128)S(6)} %select_n.145), kind=kOutput, calls=%fused_computation.3.clone.1 | convolution fusion | flops 1077934080 | bytes 1056772 | tf_op jit(solution)/shard_map/while/body/eval_jaxpr/dot_general | solution.py:46
  131.0 0.6 dynamic_slice.37
  133.6 3.4 %convolution_reduce_fusion.2 = f32[2048]{0:T(1024)S(1)} fusion(bf16[2048,128]{1,0:T(8,128)(2,1)S(1)} %get-tuple-element.119, bf16[16384,128]{1,0:T(8,128)(2,1)} %get-tuple-element.118, s32[]{:T(128)S(6)} %select_n.145), kind=kOutput, calls=%fused_computation.3.clone.1 | convolution fusion | flops 1077934080 | bytes 1056772 | tf_op jit(solution)/shard_map/while/body/eval_jaxpr/dot_general | solution.py:46
  137.0 0.6 dynamic_slice.37
  139.5 3.4 %convolution_reduce_fusion.2 = f32[2048]{0:T(1024)S(1)} fusion(bf16[2048,128]{1,0:T(8,128)(2,1)S(1)} %get-tuple-element.119, bf16[16384,128]{1,0:T(8,128)(2,1)} %get-tuple-element.118, s32[]{:T(128)S(6)} %select_n.145), kind=kOutput, calls=%fused_computation.3.clone.1 | convolution fusion | flops 1077934080 | bytes 1056772 | tf_op jit(solution)/shard_map/while/body/eval_jaxpr/dot_general | solution.py:46
  143.0 0.6 dynamic_slice.37
  145.5 3.4 %convolution_reduce_fusion.2 = f32[2048]{0:T(1024)S(1)} fusion(bf16[2048,128]{1,0:T(8,128)(2,1)S(1)} %get-tuple-element.119, bf16[16384,128]{1,0:T(8,128)(2,1)} %get-tuple-element.118, s32[]{:T(128)S(6)} %select_n.145), kind=kOutput, calls=%fused_computation.3.clone.1 | convolution fusion | flops 1077934080 | bytes 1056772 | tf_op jit(solution)/shard_map/while/body/eval_jaxpr/dot_general | solution.py:46
  149.0 0.6 dynamic_slice.37
  151.5 3.4 %convolution_reduce_fusion.2 = f32[2048]{0:T(1024)S(1)} fusion(bf16[2048,128]{1,0:T(8,128)(2,1)S(1)} %get-tuple-element.119, bf16[16384,128]{1,0:T(8,128)(2,1)} %get-tuple-element.118, s32[]{:T(128)S(6)} %select_n.145), kind=kOutput, calls=%fused_computation.3.clone.1 | convolution fusion | flops 1077934080 | bytes 1056772 | tf_op jit(solution)/shard_map/while/body/eval_jaxpr/dot_general | solution.py:46
  154.9 0.6 dynamic_slice.37
  157.5 3.4 %convolution_reduce_fusion.2 = f32[2048]{0:T(1024)S(1)} fusion(bf16[2048,128]{1,0:T(8,128)(2,1)S(1)} %get-tuple-element.119, bf16[16384,128]{1,0:T(8,128)(2,1)} %get-tuple-element.118, s32[]{:T(128)S(6)} %select_n.145), kind=kOutput, calls=%fused_computation.3.clone.1 | convolution fusion | flops 1077934080 | bytes 1056772 | tf_op jit(solution)/shard_map/while/body/eval_jaxpr/dot_general | solution.py:46
  160.9 0.6 dynamic_slice.37
  163.4 3.4 %convolution_reduce_fusion.2 = f32[2048]{0:T(1024)S(1)} fusion(bf16[2048,128]{1,0:T(8,128)(2,1)S(1)} %get-tuple-element.119, bf16[16384,128]{1,0:T(8,128)(2,1)} %get-tuple-element.118, s32[]{:T(128)S(6)} %select_n.145), kind=kOutput, calls=%fused_computation.3.clone.1 | convolution fusion | flops 1077934080 | bytes 1056772 | tf_op jit(solution)/shard_map/while/body/eval_jaxpr/dot_general | solution.py:46
  166.9 0.6 dynamic_slice.37
  169.4 3.4 %convolution_reduce_fusion.2 = f32[2048]{0:T(1024)S(1)} fusion(bf16[2048,128]{1,0:T(8,128)(2,1)S(1)} %get-tuple-element.119, bf16[16384,128]{1,0:T(8,128)(2,1)} %get-tuple-element.118, s32[]{:T(128)S(6)} %select_n.145), kind=kOutput, calls=%fused_computation.3.clone.1 | convolution fusion | flops 1077934080 | bytes 1056772 | tf_op jit(solution)/shard_map/while/body/eval_jaxpr/dot_general | solution.py:46
  172.9 72.1 %pmax.7 = f32[16,4,32]{2,1,0:T(4,128)S(1)} all-reduce(f32[16,4,32]{2,1,0:T(4,128)S(1)} %reshape.168), channel_id=1, replica_groups=mesh['cent'=16,'pass'=16] {'cent'}, use_global_device_ids=true, to_apply=%region_3.4 | all-reduce | flops 2048 | bytes 16384 | tf_op jit(solution)/shard_map/pmax | solution.py:70
  245.1 0.4 convolution_select_fusion
  245.5 70.5 %psum.14 = f32[16,4,32,4]{2,3,1,0:T(4,128)S(1)} all-reduce(f32[16,4,32,4]{2,3,1,0:T(4,128)S(1)} %bitcast.44), channel_id=1, replica_groups=mesh['cent'=16,'pass'=16] {'cent'}, use_global_device_ids=true, to_apply=%region_4.5 | all-reduce | flops 8192 | bytes 65536 | tf_op jit(solution)/shard_map/psum | solution.py:71
  316.0 0.6 dynamic-slice_bitcast_fusion.1
  316.6 0.6 dynamic-slice_bitcast_fusion
  317.2 0.8 copy.55
  317.9 1.3 reshape.204
  319.2 1.9 convolution_bitcast_fusion
  321.2 0.6 copy.52
  321.8 3.2 reshape.173
  325.0 4.5 %reduce_max.18 = f32[4,32,16,3]{3,2,1,0:T(8,128)S(1)} reduce(f32[4,32,16,3,30]{4,3,2,1,0:T(4,128)} %reshape.173, f32[]{:T(128)} %constant.117.clone.1), dimensions={4}, to_apply=%region_12.13 | reduce | flops 178176 | bytes 761860 | tf_op jit(solution)/shard_map/reduce_max | solution.py:105
  329.8 0.7 broadcast_select_fusion.1
  (70 shorter events, 2.8 us)
Async XLA Ops:
  7.2 6.7 %copy-start.6 = (s32[384]{0:T(512)S(1)}, s32[384]{0:T(512)}, u32[]{:S(2)}) copy-start(s32[384]{0:T(512)} %param.17) | copy-start | bytes 4612
  7.2 6.7 %copy-start.7 = (s32[4,40]{1,0:T(4,128)S(1)}, s32[4,40]{1,0:T(4,128)}, u32[]{:S(2)}) copy-start(s32[4,40]{1,0:T(4,128)} %param.18) | copy-start | bytes 1924
  7.2 6.9 %copy-start.8 = (s32[4]{0:T(128)S(1)}, s32[4]{0:T(128)}, u32[]{:S(2)}) copy-start(s32[4]{0:T(128)} %param.19) | copy-start | bytes 52
  7.2 17.2 %copy-start.3 = (s32[24,2,128]{2,1,0:T(2,128)S(1)}, s32[24,2,128]{2,1,0:T(2,128)}, u32[]{:S(2)}) copy-start(s32[24,2,128]{2,1,0:T(2,128)} %param.16) | copy-start | bytes 73732
  7.2 17.3 %copy-start.4 = (s32[1024,4]{0,1:T(4,128)S(1)}, s32[1024,4]{0,1:T(4,128)}, u32[]{:S(2)}) copy-start(s32[1024,4]{0,1:T(4,128)} %param.12) | copy-start | bytes 49156
  7.2 103.0 %all-reduce.2.cloned.1.call-start = ((), (), s32[]{:S(2)}) async-start(), calls=%async_computation.2 | async-start | bytes 368640 | tf_op jit(solution)/shard_map/psum | solution.py:69
  12.6 17.9 %copy-start.1 = (bf16[4,32,128]{2,1,0:T(8,128)(2,1)S(1)}, bf16[4,32,128]{2,1,0:T(8,128)(2,1)}, u32[]{:S(2)}) copy-start(bf16[4,32,128]{2,1,0:T(8,128)(2,1)} %param.11) | copy-start | bytes 98308
  13.8 43.1 %copy-start.5 = (f32[4,128]{1,0:T(4,128)S(1)}, f32[4,128]{1,0:T(4,128)}, u32[]{:S(2)}) copy-start(f32[4,128]{1,0:T(4,128)} %param.14) | copy-start | bytes 6148
  15.8 41.5 %all-to-all-start = ((s32[16,4,3]{2,1,0:T(4,128)}), s32[16,4,3]{2,1,0:T(4,128)S(1)}, u32[]{:S(2)}, u32[]{:S(2)}) async-start(s32[16,4,3]{2,1,0:T(4,128)} %copy.43), calls=%async_computation | async-start | bytes 65536 | tf_op jit(solution)/shard_map/all_to_all | solution.py:97
  117.4 7.6 %copy-start = (bf16[64,32,128]{2,1,0:T(8,128)(2,1)S(1)}, bf16[64,32,128]{2,1,0:T(8,128)(2,1)}, u32[]{:S(2)}) copy-start(bf16[64,32,128]{2,1,0:T(8,128)(2,1)} %all_gather.3) | copy-start | bytes 1572868
  117.4 199.8 %all-to-all-start.1 = ((bf16[16,4,3,3840]{3,1,2,0:T(4,128)(2,1)}), bf16[16,4,3,3840]{3,1,2,0:T(4,128)(2,1)S(1)}, u32[]{:S(2)}, u32[]{:S(2)}) async-start(bf16[16,4,3,3840]{3,1,2,0:T(4,128)(2,1)} %copy.49), calls=%async_computation.1 | async-start | bytes 2949120 | tf_op jit(solution)/shard_map/all_to_all | solution.py:100
  125.0 120.0 %copy-start.2 = (bf16[256,128]{1,0:T(8,128)(2,1)S(1)}, bf16[256,128]{1,0:T(8,128)(2,1)}, u32[]{:S(2)}) copy-start(bf16[256,128]{1,0:T(8,128)(2,1)} %gather_fusion) | copy-start | bytes 196612
Sparse Core Ops, SparseCore 0:
  14.0 96.2 all-reduce.1
where the time goes:
time: 338 us; the launch traced here: 337 us
  blocking collectives  169 us (50%)
  waiting for transfers between devices  52.8 us (16%)
  matrix products  29.6 us (9%)
  local copies, waits for them, and re-layouts  27.2 us (8%)
  starting transfers between devices  16.2 us (5%)
  loops' own time  15.8 us (5%)
  between operations  14.4 us (4%)
  other arithmetic  12.4 us (4%)
    pmax x1, blocking collectives, body(): best_all = lax.pmax(running, 'cent')  72.1 us
    psum x1, blocking collectives, body(): probe_all = lax.psum(jnp.where(inside_mask, probe_terms, 0.0), 'cent')  70.5 us
    psum x1, waiting for transfers between devices, body(): lax.psum(cell_terms.astype(jnp.bfloat16), 'cent').astype(jnp.float32)  52.8 us
    dot_general x8, matrix products, scan_block(): lax.dot_general(flattened, block_rows, (((1,), (1,)), ((), ())), preferre...  27.2 us
    all_gather x1, blocking collectives, body(): grouped = lax.all_gather(queries, 'cent', axis=0, tiled=True)  26.3 us
    another operation x1, loops' own time, body(): lax.scan(scan_block, jnp.full((flattened.shape[0],), -1e+30, jnp.float32)...  15.8 us
    all_to_all x1, starting transfers between devices, body(): lax.all_to_all(requests, 'pass', split_axis=0, concat_axis=0, tiled=True)  8.59 us
    all_to_all x1, starting transfers between devices, body(): lax.all_to_all(blocks, 'pass', split_axis=0, concat_axis=0, tiled=True)  7.63 us
  transfers between devices with their start and end apart: 3, of which 1 were waited for; matrix products, arithmetic and copies ran while one was open for 13% of the time, Pallas kernels for 0%

commit v1 on v0

v1 whole, which is shorter than its diff:
```python
import jax
import jax.numpy as jnp
from jax import lax
from jax.experimental import pallas as pl
from jax.experimental.pallas import tpu as pltpu
from jax.sharding import PartitionSpec as P

MESH = pl.DeviceIdType.MESH
DIM = 128
QT = 32
NPROBE = 4
PLEN = 30
P_OWN = 24
CMAX = 40
NC = 16
NP = 16
QD = 4
TOK = QD * QT
SHARD = 16384
SHIFT = 14
CHUNK = 4096
TILE = 512
ROWS = 80
F32 = jnp.float32
BF16 = jnp.bfloat16


def ahead(c, d):
    y = lax.rem(lax.div(c, 4) + lax.div(d, 4), 4)
    x = lax.rem(lax.rem(c, 4) + lax.rem(d, 4), 4)
    return y * 4 + x


def behind(c, d):
    y = lax.rem(lax.div(c, 4) + 4 - lax.div(d, 4), 4)
    x = lax.rem(lax.rem(c, 4) + 4 - lax.rem(d, 4), 4)
    return y * 4 + x


def kernel(
    q_ref, probes, cells, codes, book, locations, candidates, lengths, cent_hbm,
    top_out, probe_out, score_out,
    cent, queries, row_send, row_recv, passages, sim_send, sim_recv, top_send, top_recv, where_at,
    load_sem, qs, qr, rs, rr, ps, pr, ss, sr, ts, tr,
):
    c = lax.axis_index("cent")
    p = lax.axis_index("pass")

    loads = [
        pltpu.make_async_copy(
            cent_hbm.at[pl.ds(i * CHUNK // 16, CHUNK // 16)], cent.at[pl.ds(i * CHUNK // 16, CHUNK // 16)], load_sem.at[i]
        )
        for i in range(SHARD // CHUNK)
    ]
    for load in loads:
        load.start()

    barrier = pltpu.get_barrier_semaphore()

    def greet(d, carry):
        pl.semaphore_signal(barrier, inc=1, device_id=(ahead(c, d), p), device_id_type=MESH)
        pl.semaphore_signal(barrier, inc=1, device_id=(c, lax.rem(p + d, NP)), device_id_type=MESH)
        return carry

    lax.fori_loop(1, 16, greet, 0)
    queries[pl.ds(0, TOK), :] = q_ref[...]

    lane8 = lax.broadcasted_iota(jnp.int32, (8, 128), 1)
    sub8 = lax.broadcasted_iota(jnp.int32, (8, 128), 0)
    for q in range(QD):
        found = jnp.full((8, 128), -1, jnp.int32)
        for slot in range(CMAX):
            found = jnp.where(lane8 == slot, locations[candidates[q, slot]], found)
        where_at[q] = jnp.where(lane8 < lengths[q], found, -1)

    pl.semaphore_wait(barrier, 30)

    def to_cent(src, dst, d, send, recv, target):
        return pltpu.make_async_remote_copy(
            src_ref=src, dst_ref=dst, send_sem=send.at[d], recv_sem=recv.at[d],
            device_id=(target, p), device_id_type=MESH,
        )

    def query_copy(d):
        return to_cent(
            queries.at[pl.ds(0, TOK)], queries.at[pl.ds(pl.multiple_of(d * TOK, TOK), TOK)], d, qs, qr, ahead(c, d)
        )

    def row_copy(d):
        return to_cent(row_send.at[d], row_recv.at[d], d, rs, rr, ahead(c, d))

    def passage_copy(d):
        return pltpu.make_async_remote_copy(
            src_ref=passages.at[0], dst_ref=passages.at[d], send_sem=ps.at[d], recv_sem=pr.at[d],
            device_id=(c, lax.rem(p + d, NP)), device_id_type=MESH,
        )

    def sim_copy(d):
        return to_cent(sim_send.at[d], sim_recv.at[d], d, ss, sr, behind(c, d))

    def top_copy(d):
        return to_cent(top_send.at[d], top_recv.at[d], d, ts, tr, behind(c, d))

    def send_queries(d, carry):
        query_copy(d).start()
        return carry

    lax.fori_loop(1, NC, send_queries, 0)
    for load in loads:
        load.wait()

    mine = [jnp.where(sub8 == r, c, -1) for r in range(8)]

    def pick(ids):
        parts = []
        for base in range(0, len(ids), 8):
            acc = jnp.zeros((8, DIM), F32)
            for r, i in enumerate(ids[base : base + 8]):
                pair = cent[(i & (SHARD - 1)) >> 4].astype(F32)
                ids_r = jnp.full((8, DIM), i, jnp.int32)
                half = jnp.where((ids_r & 8) != 0, pair[8:], pair[:8])
                row = jnp.take_along_axis(half, ids_r & 7, axis=0)
                acc = jnp.where(mine[r] == (ids_r >> SHIFT), row, acc)
            parts.append(acc)
        return jnp.concatenate(parts, axis=0).astype(BF16)

    def collect(d, carry):
        target = ahead(c, d)
        second = P_OWN - 8 + lax.div(target, 2)
        row_send[d, pl.ds(0, 32), :] = pick([cells[target, min(j, PLEN - 1)] for j in range(32)])
        row_send[d, pl.ds(32, 32), :] = pick([cells[second, min(j, PLEN - 1)] for j in range(32)])
        first = (target * NP + p) * QD
        row_send[d, pl.ds(64, 16), :] = pick([probes[k, first + q] for q in range(QD) for k in range(NPROBE)])

        @pl.when(d > 0)
        def _():
            row_copy(d).start()

        return carry

    lax.fori_loop(0, NC, collect, 0)

    def scan_tile(t, carry):
        tile = queries[pl.ds(pl.multiple_of(t * TILE, TILE), TILE), :]

        def step(i, best):
            rows = cent[pl.ds(i * (CHUNK // 16), CHUNK // 16)].reshape(CHUNK, DIM)
            dots = lax.dot_general(rows, tile, (((1,), (1,)), ((), ())), preferred_element_type=F32)
            return jnp.maximum(best, jnp.max(dots.reshape(CHUNK // 8, 8, TILE), axis=0))

        best = lax.fori_loop(0, SHARD // CHUNK, step, jnp.full((8, TILE), -jnp.inf, F32))
        for i in range(TILE // TOK):
            top_send[t * (TILE // TOK) + i] = best[:, i * TOK : (i + 1) * TOK]
        return carry

    def get_queries(d, carry):
        query_copy(d).wait_recv()
        return carry

    def send_tops(d, carry):
        top_copy(d).start()
        return carry

    lax.fori_loop(1, 4, get_queries, 0)
    scan_tile(0, 0)
    lax.fori_loop(1, 4, send_tops, 0)
    top_recv[0] = top_send[0]

    def get_rows(d, total):
        row_copy(d).wait_recv()
        return total + row_recv[d].astype(F32)

    rows = lax.fori_loop(1, NC, get_rows, row_send[0].astype(F32))
    own = queries[pl.ds(0, TOK), :]
    probe_dots = lax.dot_general(
        rows[64:].astype(BF16), own, (((1,), (1,)), ((), ())), preferred_element_type=F32
    )
    for q in range(QD):
        probe_out[q] = probe_dots[q * NPROBE : (q + 1) * NPROBE, q * QT : (q + 1) * QT]

    token = jnp.minimum(lax.broadcasted_iota(jnp.int32, (32, DIM), 0), PLEN - 1)
    shift = 2 * jnp.where(token >= 15, token - 15, token)
    for s, at in enumerate((c, P_OWN - 8 + lax.div(c, 2))):
        words = codes[at]
        word = jnp.where(token >= 15, words[1:2, :], words[0:1, :])
        level = jnp.right_shift(word, shift) & 3
        residual = jnp.where(
            level < 2,
            jnp.where(level == 0, book[0:1, :], book[1:2, :]),
            jnp.where(level == 2, book[2:3, :], book[3:4, :]),
        )
        vector = rows[s * 32 : (s + 1) * 32] + residual
        squares = jnp.sum(vector * vector, axis=-1, keepdims=True)
        passages[0, pl.ds(s * 32, 32), :] = (vector * lax.rsqrt(squares + 1e-06)).astype(BF16)

    def send_passages(d, carry):
        passage_copy(d).start()
        return carry

    lax.fori_loop(1, NP, send_passages, 0)

    lax.fori_loop(4, 8, get_queries, 0)
    scan_tile(1, 0)
    lax.fori_loop(4, 8, send_tops, 0)

    def get_passages(d, carry):
        passage_copy(d).wait_recv()
        return carry

    lax.fori_loop(1, NP, get_passages, 0)
    lax.fori_loop(8, NC, get_queries, 0)

    def sims(t, carry):
        tile = queries[pl.ds(pl.multiple_of(t * TILE, TILE), TILE), :]
        dots = lax.dot_general(
            passages[...].reshape(NP * 64, DIM), tile, (((1,), (1,)), ((), ())), preferred_element_type=F32
        )
        most = jnp.max(dots.reshape(32, 32, TILE), axis=1)
        for i in range(TILE // TOK):
            sim_send[t * (TILE // TOK) + i] = most[:, i * TOK : (i + 1) * TOK]
        return carry

    lax.fori_loop(0, NC * TOK // TILE, sims, 0)

    def send_sims(d, carry):
        sim_copy(d).start()
        return carry

    lax.fori_loop(1, NC, send_sims, 0)
    sim_recv[0] = sim_send[0]

    lax.fori_loop(2, 4, scan_tile, 0)
    lax.fori_loop(8, NC, send_tops, 0)

    def get_sims(d, carry):
        sim_copy(d).wait_recv()
        return carry

    lax.fori_loop(1, NC, get_sims, 0)
    groups = lax.broadcasted_iota(jnp.int32, (TOK, QD * 128), 0) // QT
    weights = jnp.where(
        groups == lax.broadcasted_iota(jnp.int32, (TOK, QD * 128), 1) // 128, 1.0 / QT, 0.0
    ).astype(BF16)
    odd = lax.rem(sub8, 2) == 1
    bases = []
    for g in range(4):
        owner = lax.rem(p + NP - (g * 4 + lax.div(sub8, 2)), NP)
        bases.append(owner * P_OWN)

    def score(d, totals):
        cc = ahead(c, d)
        m = sim_recv[d]
        high = m.astype(BF16)
        low = (m - high.astype(F32)).astype(BF16)
        means = jnp.dot(high, weights, preferred_element_type=F32) + jnp.dot(
            low, weights, preferred_element_type=F32
        )
        out = []
        for q in range(QD):
            total = totals[q]
            for g in range(4):
                position = bases[g] + jnp.where(odd, P_OWN - 8 + lax.div(cc, 2), cc)
                total = jnp.where(
                    position == where_at[q], means[g * 8 : (g + 1) * 8, q * 128 : (q + 1) * 128], total
                )
            out.append(total)
        return tuple(out)

    totals = lax.fori_loop(0, NC, score, tuple(jnp.zeros((8, 128), F32) for _ in range(QD)))
    for q in range(QD):
        score_out[pl.ds(q, 1), :] = jnp.sum(totals[q], axis=0, keepdims=True)[:, :CMAX]

    def get_tops(d, best):
        top_copy(d).wait_recv()
        return jnp.maximum(best, top_recv[d])

    best = lax.fori_loop(1, NC, get_tops, top_recv[0])
    best = jnp.max(best, axis=0, keepdims=True)
    for q in range(QD):
        top_out[pl.ds(q, 1), :] = best[:, q * QT : (q + 1) * QT]

    def finish(d, carry):
        query_copy(d).wait_send()
        row_copy(d).wait_send()
        passage_copy(d).wait_send()
        sim_copy(d).wait_send()
        top_copy(d).wait_send()
        return carry

    lax.fori_loop(1, NC, finish, 0)


def body(queries, probes, centroids, codebook, token_cells, codes, locations, candidates, lengths):
    vmem = pl.BlockSpec(memory_space=pltpu.VMEM)
    smem = pl.BlockSpec(memory_space=pltpu.SMEM)
    sems = pltpu.SemaphoreType.DMA((NC,))
    top, probe, score = pl.pallas_call(
        kernel,
        out_shape=(
            jax.ShapeDtypeStruct((QD, QT), F32),
            jax.ShapeDtypeStruct((QD, NPROBE, QT), F32),
            jax.ShapeDtypeStruct((QD, CMAX), F32),
        ),
        in_specs=[vmem, smem, smem, vmem, vmem, smem, smem, smem, pl.BlockSpec(memory_space=pl.ANY)],
        out_specs=(vmem, vmem, vmem),
        scratch_shapes=[
            pltpu.VMEM((SHARD // 16, 16, DIM), BF16),
            pltpu.VMEM((NC * TOK, DIM), BF16),
            pltpu.VMEM((NC, ROWS, DIM), BF16),
            pltpu.VMEM((NC, ROWS, DIM), BF16),
            pltpu.VMEM((NP, 64, DIM), BF16),
            pltpu.VMEM((NC, 32, TOK), F32),
            pltpu.VMEM((NC, 32, TOK), F32),
            pltpu.VMEM((NC, 8, TOK), F32),
            pltpu.VMEM((NC, 8, TOK), F32),
            pltpu.VMEM((QD, 8, 128), jnp.int32),
            pltpu.SemaphoreType.DMA((SHARD // CHUNK,)),
        ]
        + [sems] * 10,
        compiler_params=pltpu.CompilerParams(
            collective_id=0, has_side_effects=True, vmem_limit_bytes=48 << 20
        ),
        name="late_interaction",
    )(
        queries.reshape(TOK, DIM), probes.T, token_cells, codes, codebook, locations, candidates, lengths,
        centroids.reshape(SHARD // 16, 16, DIM),
    )
    return top, jnp.transpose(probe, (0, 2, 1)), score


def solution(mesh):
    placed = (
        P(("cent", "pass"), None, None),
        P(),
        P("cent", None),
        P(),
        P("pass", None),
        P("pass", None, None),
        P(),
        P(("cent", "pass"), None),
        P(("cent", "pass")),
    )
    return jax.shard_map(
        body,
        mesh=mesh,
        in_specs=placed,
        out_specs=(
            P(("cent", "pass"), None),
            P(("cent", "pass"), None, None),
            P(("cent", "pass"), None),
        ),
        check_vma=False,
    )
```

time: 338 us -> 61.2 us (0.18)
  the two profiles are of different devices: /device:TPU:32 before, /device:TPU:1 now
where the time goes in v1:
time: 61.2 us; the launch traced here: 60.8 us
  Pallas kernels  50.6 us (83%)
  local copies, waits for them, and re-layouts  9.55 us (16%)
  between operations  0.66 us (1%)
    pallas_call x1, Pallas kernels, body(): pl.pallas_call(kernel, out_shape=(jax.ShapeDtypeStruct((QD, QT), F32), ja...  50.6 us
    unnamed x21, local copies, waits for them, and re-layouts  9.55 us

profile of v1, /device:TPU:1, one launch (start us, length us, event | category | flops | bytes accessed | tf_op | source)
XLA Modules:
  0.0 60.8 jit_solution(14435931924401395743)
XLA Ops:
  0.6 0.0 copy-start
  0.6 2.2 %copy-done = bf16[16384,128]{1,0:T(8,128)(2,1)S(1)} copy-done((bf16[16384,128]{1,0:T(8,128)(2,1)S(1)}, bf16[16384,128]{1,0:T(8,128)(2,1)}, u32[]{:S(2)}) %copy-start) | copy-done | bytes 4194328
  2.8 0.0 copy-start.1
  2.8 0.8 %copy-done.1 = bf16[4,32,128]{2,1,0:T(8,128)(2,1)S(1)} copy-done((bf16[4,32,128]{2,1,0:T(8,128)(2,1)S(1)}, bf16[4,32,128]{2,1,0:T(8,128)(2,1)}, u32[]{:S(2)}) %copy-start.1) | copy-done | bytes 32792
  3.6 0.0 copy-start.2
  3.6 0.7 %copy-done.2 = s32[24,2,128]{2,1,0:T(2,128)S(1)} copy-done((s32[24,2,128]{2,1,0:T(2,128)S(1)}, s32[24,2,128]{2,1,0:T(2,128)}, u32[]{:S(2)}) %copy-start.2) | copy-done | bytes 24600
  4.3 0.0 copy-start.3
  4.3 0.7 %copy-done.3 = s32[1024,4]{0,1:T(4,128)S(1)} copy-done((s32[1024,4]{0,1:T(4,128)S(1)}, s32[1024,4]{0,1:T(4,128)}, u32[]{:S(2)}) %copy-start.3) | copy-done | bytes 16408
  5.0 0.0 copy-start.4
  5.0 0.7 %copy-done.4 = s32[24,30]{1,0:T(8,128)S(1)} copy-done((s32[24,30]{1,0:T(8,128)S(1)}, s32[24,30]{1,0:T(8,128)}, u32[]{:S(2)}) %copy-start.4) | copy-done | bytes 2904
  5.7 0.0 copy-start.5
  5.7 0.7 %copy-done.5 = f32[4,128]{1,0:T(4,128)S(1)} copy-done((f32[4,128]{1,0:T(4,128)S(1)}, f32[4,128]{1,0:T(4,128)}, u32[]{:S(2)}) %copy-start.5) | copy-done | bytes 2072
  6.4 0.0 copy-start.6
  6.4 0.7 %copy-done.6 = s32[384]{0:T(512)S(1)} copy-done((s32[384]{0:T(512)S(1)}, s32[384]{0:T(512)}, u32[]{:S(2)}) %copy-start.6) | copy-done | bytes 1560
  7.1 0.0 copy-start.7
  7.1 0.7 %copy-done.7 = s32[4,40]{1,0:T(4,128)S(1)} copy-done((s32[4,40]{1,0:T(4,128)S(1)}, s32[4,40]{1,0:T(4,128)}, u32[]{:S(2)}) %copy-start.7) | copy-done | bytes 664
  7.8 0.0 copy-start.8
  7.8 0.7 %copy-done.8 = s32[4]{0:T(128)S(1)} copy-done((s32[4]{0:T(128)S(1)}, s32[4]{0:T(128)}, u32[]{:S(2)}) %copy-start.8) | copy-done | bytes 40
  8.4 50.6 %late_interaction.1 = (f32[4,32]{1,0:T(4,128)S(1)}, f32[4,4,32]{2,1,0:T(4,128)S(1)}, f32[4,40]{1,0:T(4,128)S(1)}) custom-call(bf16[128,128]{1,0:T(8,128)(2,1)S(1)} %bitcast.5, s32[4,1024]{1,0:T(4,128)S(1)} %bitcast.6, s32[24,30]{1,0:T(8,128)S(1)} %copy-done.4, s32[24,2,128]{2,1,0:T(2,128)S(1)} %copy-done.2, f32[4,128]{1,0:T(4,128)S(1)} %copy-done.5, ...), custom_call_target="tpu_custom_call" | custom-call | tf_op jit(solution)/shard_map/late_interaction/pallas_call | solution.py:297
  59.0 0.6 copy.15
  59.6 0.6 copy.16
  60.2 0.6 copy.17
Async XLA Ops:
  0.6 2.2 %copy-start = (bf16[16384,128]{1,0:T(8,128)(2,1)S(1)}, bf16[16384,128]{1,0:T(8,128)(2,1)}, u32[]{:S(2)}) copy-start(bf16[16384,128]{1,0:T(8,128)(2,1)} %param.11) | copy-start | bytes 12582916
  2.8 0.8 %copy-start.1 = (bf16[4,32,128]{2,1,0:T(8,128)(2,1)S(1)}, bf16[4,32,128]{2,1,0:T(8,128)(2,1)}, u32[]{:S(2)}) copy-start(bf16[4,32,128]{2,1,0:T(8,128)(2,1)} %param.9) | copy-start | bytes 98308
  3.6 0.7 %copy-start.2 = (s32[24,2,128]{2,1,0:T(2,128)S(1)}, s32[24,2,128]{2,1,0:T(2,128)}, u32[]{:S(2)}) copy-start(s32[24,2,128]{2,1,0:T(2,128)} %codes.1) | copy-start | bytes 73732
  4.3 0.7 %copy-start.3 = (s32[1024,4]{0,1:T(4,128)S(1)}, s32[1024,4]{0,1:T(4,128)}, u32[]{:S(2)}) copy-start(s32[1024,4]{0,1:T(4,128)} %param.10) | copy-start | bytes 49156
  5.0 0.7 %copy-start.4 = (s32[24,30]{1,0:T(8,128)S(1)}, s32[24,30]{1,0:T(8,128)}, u32[]{:S(2)}) copy-start(s32[24,30]{1,0:T(8,128)} %cells.1) | copy-start | bytes 8644
  5.7 0.7 %copy-start.5 = (f32[4,128]{1,0:T(4,128)S(1)}, f32[4,128]{1,0:T(4,128)}, u32[]{:S(2)}) copy-start(f32[4,128]{1,0:T(4,128)} %book.1) | copy-start | bytes 6148
  6.4 0.7 %copy-start.6 = (s32[384]{0:T(512)S(1)}, s32[384]{0:T(512)}, u32[]{:S(2)}) copy-start(s32[384]{0:T(512)} %locations.1) | copy-start | bytes 4612
  7.1 0.7 %copy-start.7 = (s32[4,40]{1,0:T(4,128)S(1)}, s32[4,40]{1,0:T(4,128)}, u32[]{:S(2)}) copy-start(s32[4,40]{1,0:T(4,128)} %candidates.1) | copy-start | bytes 1924
  7.8 0.7 %copy-start.8 = (s32[4]{0:T(128)S(1)}, s32[4]{0:T(128)}, u32[]{:S(2)}) copy-start(s32[4]{0:T(128)} %lengths.1) | copy-start | bytes 52

commit v2 on v1

--- a/solution.py
+++ b/solution.py
@@ -38,10 +38,11 @@
 
 
 def kernel(
-    q_ref, probes, cells, codes, book, locations, candidates, lengths, cent_hbm,
+    q_hbm, probes_hbm, cells_hbm, codes_hbm, book_hbm, locations_hbm, candidates_hbm, lengths_hbm, cent_hbm,
     top_out, probe_out, score_out,
+    probes, cells, codes, book, locations, candidates, lengths,
     cent, queries, row_send, row_recv, passages, sim_send, sim_recv, top_send, top_recv, where_at,
-    load_sem, qs, qr, rs, rr, ps, pr, ss, sr, ts, tr,
+    load_sem, small_sem, qs, qr, rs, rr, ps, pr, ss, sr, ts, tr,
 ):
     c = lax.axis_index("cent")
     p = lax.axis_index("pass")
@@ -52,7 +53,22 @@
         )
         for i in range(SHARD // CHUNK)
     ]
-    for load in loads:
+    small = [
+        pltpu.make_async_copy(src, dst, small_sem.at[i])
+        for i, (src, dst) in enumerate(
+            (
+                (q_hbm, queries.at[pl.ds(0, TOK)]),
+                (cells_hbm, cells),
+                (probes_hbm, probes),
+                (codes_hbm, codes),
+                (book_hbm, book),
+                (locations_hbm, locations),
+                (candidates_hbm, candidates),
+                (lengths_hbm, lengths),
+            )
+        )
+    ]
+    for load in small + loads:
         load.start()
 
     barrier = pltpu.get_barrier_semaphore()
@@ -63,17 +79,12 @@
         return carry
 
     lax.fori_loop(1, 16, greet, 0)
-    queries[pl.ds(0, TOK), :] = q_ref[...]
-
-    lane8 = lax.broadcasted_iota(jnp.int32, (8, 128), 1)
+
+    pl.semaphore_wait(barrier, 30)
+
+    for load in small:
+        load.wait()
     sub8 = lax.broadcasted_iota(jnp.int32, (8, 128), 0)
-    for q in range(QD):
-        found = jnp.full((8, 128), -1, jnp.int32)
-        for slot in range(CMAX):
-            found = jnp.where(lane8 == slot, locations[candidates[q, slot]], found)
-        where_at[q] = jnp.where(lane8 < lengths[q], found, -1)
-
-    pl.semaphore_wait(barrier, 30)
 
     def to_cent(src, dst, d, send, recv, target):
         return pltpu.make_async_remote_copy(
@@ -105,7 +116,7 @@
         query_copy(d).start()
         return carry
 
-    lax.fori_loop(1, NC, send_queries, 0)
+    lax.fori_loop(1, 4, send_queries, 0)
     for load in loads:
         load.wait()
 
@@ -139,6 +150,14 @@
         return carry
 
     lax.fori_loop(0, NC, collect, 0)
+    lax.fori_loop(4, NC, send_queries, 0)
+
+    lane8 = lax.broadcasted_iota(jnp.int32, (8, 128), 1)
+    for q in range(QD):
+        found = jnp.full((8, 128), -1, jnp.int32)
+        for slot in range(CMAX):
+            found = jnp.where(lane8 == slot, locations[candidates[q, slot]], found)
+        where_at[q] = jnp.where(lane8 < lengths[q], found, -1)
 
     def scan_tile(t, carry):
         tile = queries[pl.ds(pl.multiple_of(t * TILE, TILE), TILE), :]
@@ -203,12 +222,16 @@
     scan_tile(1, 0)
     lax.fori_loop(4, 8, send_tops, 0)
 
+    lax.fori_loop(8, 12, get_queries, 0)
+    scan_tile(2, 0)
+    lax.fori_loop(8, 12, send_tops, 0)
+
     def get_passages(d, carry):
         passage_copy(d).wait_recv()
         return carry
 
     lax.fori_loop(1, NP, get_passages, 0)
-    lax.fori_loop(8, NC, get_queries, 0)
+    lax.fori_loop(12, NC, get_queries, 0)
 
     def sims(t, carry):
         tile = queries[pl.ds(pl.multiple_of(t * TILE, TILE), TILE), :]
@@ -229,8 +252,8 @@
     lax.fori_loop(1, NC, send_sims, 0)
     sim_recv[0] = sim_send[0]
 
-    lax.fori_loop(2, 4, scan_tile, 0)
-    lax.fori_loop(8, NC, send_tops, 0)
+    scan_tile(3, 0)
+    lax.fori_loop(12, NC, send_tops, 0)
 
     def get_sims(d, carry):
         sim_copy(d).wait_recv()
@@ -290,20 +313,32 @@
     lax.fori_loop(1, NC, finish, 0)
 
 
+def deliver(top, probe, score, top_out, probe_out, score_out):
+    top_out[...] = top[...]
+    probe_out[...] = probe[...]
+    score_out[...] = score[...]
+
+
 def body(queries, probes, centroids, codebook, token_cells, codes, locations, candidates, lengths):
     vmem = pl.BlockSpec(memory_space=pltpu.VMEM)
-    smem = pl.BlockSpec(memory_space=pltpu.SMEM)
     sems = pltpu.SemaphoreType.DMA((NC,))
-    top, probe, score = pl.pallas_call(
+    results = pl.pallas_call(
         kernel,
         out_shape=(
             jax.ShapeDtypeStruct((QD, QT), F32),
             jax.ShapeDtypeStruct((QD, NPROBE, QT), F32),
             jax.ShapeDtypeStruct((QD, CMAX), F32),
         ),
-        in_specs=[vmem, smem, smem, vmem, vmem, smem, smem, smem, pl.BlockSpec(memory_space=pl.ANY)],
+        in_specs=[pl.BlockSpec(memory_space=pltpu.HBM)] * 9,
         out_specs=(vmem, vmem, vmem),
         scratch_shapes=[
+            pltpu.SMEM((NPROBE, NC * NP * QD), jnp.int32),
+            pltpu.SMEM((P_OWN, PLEN), jnp.int32),
+            pltpu.VMEM((P_OWN, 2, DIM), jnp.int32),
+            pltpu.VMEM((4, DIM), F32),
+            pltpu.SMEM((NP * P_OWN,), jnp.int32),
+            pltpu.SMEM((QD, CMAX), jnp.int32),
+            pltpu.SMEM((QD,), jnp.int32),
             pltpu.VMEM((SHARD // 16, 16, DIM), BF16),
             pltpu.VMEM((NC * TOK, DIM), BF16),
             pltpu.VMEM((NC, ROWS, DIM), BF16),
@@ -315,16 +350,24 @@
             pltpu.VMEM((NC, 8, TOK), F32),
             pltpu.VMEM((QD, 8, 128), jnp.int32),
             pltpu.SemaphoreType.DMA((SHARD // CHUNK,)),
+            pltpu.SemaphoreType.DMA((8,)),
         ]
         + [sems] * 10,
         compiler_params=pltpu.CompilerParams(
-            collective_id=0, has_side_effects=True, vmem_limit_bytes=48 << 20
+            collective_id=0, has_side_effects=True, vmem_limit_bytes=60 << 20
         ),
         name="late_interaction",
     )(
         queries.reshape(TOK, DIM), probes.T, token_cells, codes, codebook, locations, candidates, lengths,
         centroids.reshape(SHARD // 16, 16, DIM),
     )
+    top, probe, score = pl.pallas_call(
+        deliver,
+        out_shape=tuple(jax.ShapeDtypeStruct(r.shape, r.dtype) for r in results),
+        in_specs=[vmem] * 3,
+        out_specs=[vmem] * 3,
+        name="deliver",
+    )(*results)
     return top, jnp.transpose(probe, (0, 2, 1)), score
 
 

time: 61.2 us -> 48.4 us (0.79)
  local copies, waits for them, and re-layouts: 9.55 us -> 0 us
  Pallas kernels: 50.6 us -> 47.6 us
    unnamed x21 -> x0, local copies, waits for them, and re-layouts: 9.55 us -> none
    pallas_call x1, Pallas kernels: 50.6 us -> 46.3 us  [body(): pl.pallas_call(kernel, out_shape=(jax.ShapeDtypeStruct((QD, QT), F32), ja...]
    pallas_call x0 -> x1, Pallas kernels: none -> 1.3 us  [body(): pl.pallas_call(deliver, out_shape=tuple((jax.ShapeDtypeStruct(r.shape, r....]
where the time goes in v2:
time: 48.4 us; the launch traced here: 48.2 us
  Pallas kernels  47.6 us (98%)
  between operations  0.64 us (1%)
    pallas_call x1, Pallas kernels, body(): pl.pallas_call(kernel, out_shape=(jax.ShapeDtypeStruct((QD, QT), F32), ja...  46.3 us
    pallas_call x1, Pallas kernels, body(): pl.pallas_call(deliver, out_shape=tuple((jax.ShapeDtypeStruct(r.shape, r....  1.3 us

profile of v2, /device:TPU:1, one launch (start us, length us, event | category | flops | bytes accessed | tf_op | source)
XLA Modules:
  0.0 48.2 jit_solution(3124201457904653650)
XLA Ops:
  0.6 46.3 %late_interaction.1 = (f32[4,32]{1,0:T(4,128)}, f32[4,4,32]{2,1,0:T(4,128)}, f32[4,40]{1,0:T(4,128)}) custom-call(bf16[128,128]{1,0:T(8,128)(2,1)} %bitcast.5, s32[4,1024]{1,0:T(4,128)} %bitcast.6, s32[24,30]{1,0:T(8,128)} %cells_hbm.1, s32[24,2,128]{2,1,0:T(2,128)} %codes_hbm.1, f32[4,128]{1,0:T(4,128)} %book_hbm.1, s32[384]{0:T(512)} %locations_hbm.1, ...), custom_call_target="tpu_custom_call" | custom-call | tf_op jit(solution)/shard_map/late_interaction/pallas_call | solution.py:325
  46.9 1.3 %deliver.1 = (f32[4,32]{1,0:T(4,128)}, f32[4,4,32]{2,1,0:T(4,128)}, f32[4,40]{1,0:T(4,128)}) custom-call(f32[4,32]{1,0:T(4,128)} %get-tuple-element.9.top, f32[4,4,32]{2,1,0:T(4,128)} %get-tuple-element.10.probe, f32[4,40]{1,0:T(4,128)} %get-tuple-element.11.score), custom_call_target="tpu_custom_call" | custom-call | tf_op jit(solution)/shard_map/deliver/pallas_call | solution.py:364

commit v3 on v2

v3 whole, which is shorter than its diff:
```python
import jax
import jax.numpy as jnp
from jax import lax
from jax.experimental import pallas as pl
from jax.experimental.pallas import tpu as pltpu
from jax.sharding import PartitionSpec as P

MESH = pl.DeviceIdType.MESH
DIM = 128
QT = 32
NPROBE = 4
PLEN = 30
P_OWN = 24
CMAX = 40
NC = 16
NP = 16
QD = 4
TOK = QD * QT
SHARD = 16384
SHIFT = 14
CHUNK = 4096
TILE = 512
STEPS = SHARD // CHUNK
EVEN = 8 * 64
F32 = jnp.float32
BF16 = jnp.bfloat16


def kernel(
    q_hbm, probes_hbm, cells_hbm, codes_hbm, book_hbm, locations_hbm, candidates_hbm, lengths_hbm, cent_hbm,
    top_out, probe_out, score_out,
    probes, cells, codes, book, locations, candidates, lengths,
    cent, queries, first_send, first_recv, second_send, second_recv, column_send, column_recv, late_send, late_recv,
    probed, passages, result_send, result_recv, wanted, running,
    load_sem, small_sem, qs, qr, ws, wr, vs, vr, us, ur,
):
    c = lax.axis_index("cent")
    p = lax.axis_index("pass")
    y, x = lax.div(c, 4), lax.rem(c, 4)
    z, core = lax.div(p, 2), lax.rem(p, 2)
    odd = lax.rem(c + p, 2)
    second_of = P_OWN - 8 + lax.div(c, 2)

    def cent_at(dy, dx):
        return lax.rem(y + dy, 4) * 4 + lax.rem(x + dx, 4)

    def pass_at(dz):
        return lax.rem(z + dz, 8) * 2 + core

    other = z * 2 + 1 - core

    loads = [
        pltpu.make_async_copy(
            cent_hbm.at[pl.ds(i * CHUNK // 16, CHUNK // 16)], cent.at[pl.ds(i * CHUNK // 16, CHUNK // 16)], load_sem.at[i]
        )
        for i in range(SHARD // CHUNK)
    ]
    small = [
        pltpu.make_async_copy(src, dst, small_sem.at[i])
        for i, (src, dst) in enumerate(
            (
                (q_hbm, queries.at[pl.ds(0, TOK)]),
                (cells_hbm, cells),
                (probes_hbm, probes),
                (codes_hbm, codes),
                (book_hbm, book),
                (locations_hbm, locations),
                (candidates_hbm, candidates),
                (lengths_hbm, lengths),
            )
        )
    ]
    for load in small + loads:
        load.start()

    barrier = pltpu.get_barrier_semaphore()
    partners = (
        [(cent_at(0, d), p) for d in (1, 2, 3)]
        + [(cent_at(d, 0), p) for d in (1, 2, 3)]
        + [(c, pass_at(d)) for d in range(1, 8)]
        + [(c, other)]
    )
    for partner in partners:
        pl.semaphore_signal(barrier, inc=1, device_id=partner, device_id_type=MESH)
    pl.semaphore_wait(barrier, len(partners))
    for load in small:
        load.wait()
    lane8 = lax.broadcasted_iota(jnp.int32, (8, 128), 1)
    sub8 = lax.broadcasted_iota(jnp.int32, (8, 128), 0)

    def send(src, dst, send_sem, recv_sem, target):
        pltpu.make_async_remote_copy(
            src_ref=src, dst_ref=dst, send_sem=send_sem, recv_sem=recv_sem, device_id=target, device_id_type=MESH
        ).start()

    def arrived(ref, sem):
        pltpu.make_async_remote_copy(
            src_ref=ref, dst_ref=ref, send_sem=sem, recv_sem=sem, device_id=(c, other), device_id_type=MESH
        ).wait_recv()

    def gone(ref, sem):
        pltpu.make_async_remote_copy(
            src_ref=ref, dst_ref=ref, send_sem=sem, recv_sem=sem, device_id=(c, other), device_id_type=MESH
        ).wait_send()

    for d in (1, 3, 2):
        send(queries.at[pl.ds(0, TOK)], queries.at[pl.ds(d * TOK, TOK)], qs.at[0], qr.at[0], (cent_at(0, d), p))
    for load in loads:
        load.wait()

    mine = [jnp.where(sub8 == r, c, -1) for r in range(8)]

    def pick(ids):
        parts = []
        for base in range(0, len(ids), 8):
            acc = jnp.zeros((8, DIM), F32)
            for r, i in enumerate(ids[base : base + 8]):
                pair = cent[(i & (SHARD - 1)) >> 4].astype(F32)
                ids_r = jnp.full((8, DIM), i, jnp.int32)
                half = jnp.where((ids_r & 8) != 0, pair[8:], pair[:8])
                row = jnp.take_along_axis(half, ids_r & 7, axis=0)
                acc = jnp.where(mine[r] == (ids_r >> SHIFT), row, acc)
            parts.append(acc)
        return jnp.concatenate(parts, axis=0).astype(BF16)

    def collect_first(i, carry):
        dx, dy = lax.rem(lax.div(i, 4) + 1, 4), lax.rem(i, 4)
        target = cent_at(4 - dy, 4 - dx)
        first_send[dx, dy] = pick([cells[target, min(j, PLEN - 1)] for j in range(32)])
        return carry

    def collect_second(i, carry):
        half, dy = lax.div(i, 4), lax.rem(i, 4)
        at = P_OWN - 8 + lax.div(cent_at(4 - dy, 4 - 2 * half - odd), 2)
        second_send[half, dy] = pick([cells[at, min(j, PLEN - 1)] for j in range(32)])
        return carry

    def collect_probed(d, carry):
        base = (cent_at(4 - lax.div(d, 4), 4 - lax.rem(d, 4)) * NP + p) * QD
        probed[pl.ds(pl.multiple_of(d * 16, 16), 16), :] = pick(
            [probes[k, base + q] for q in range(QD) for k in range(NPROBE)]
        )
        return carry

    lax.fori_loop(0, 12, collect_first, 0)
    for d in (1, 3, 2):
        send(first_send.at[d], first_recv.at[d], ws.at[0], wr.at[0], (cent_at(0, 4 - d), p))
    lax.fori_loop(0, 8, collect_second, 0)

    def send_second(half, d):
        send(second_send.at[half], second_recv.at[d], ws.at[1], wr.at[1], (cent_at(0, 4 - d), p))

    @pl.when(odd == 0)
    def _():
        send_second(1, 2)

    @pl.when(odd == 1)
    def _():
        send_second(0, 1)
        send_second(1, 3)

    arrived(queries.at[pl.ds(TOK, 3 * TOK)], qr.at[0])
    for d in (1, 3, 2):
        send(queries.at[pl.ds(0, TILE)], queries.at[pl.ds(d * TILE, TILE)], qs.at[d], qr.at[d], (cent_at(d, 0), p))
    lax.fori_loop(12, 16, collect_first, 0)
    lax.fori_loop(0, NC, collect_probed, 0)

    group8 = lane8 >> 5
    for base in range(0, CMAX, 8):
        found = jnp.full((8, 128), -1, jnp.int32)
        for q in range(QD):
            for r in range(8):
                at = locations[candidates[q, base + r]]
                found = jnp.where((sub8 == r) & (group8 == q), at, found)
            live = base + sub8 < lengths[q]
            found = jnp.where((group8 == q) & jnp.logical_not(live), -1, found)
        wanted[pl.ds(base, 8), :] = found

    def sum_rows():
        arrived(first_recv.at[pl.ds(1, 3)], wr.at[0])
        for dy in range(4):
            total = first_send[0, dy].astype(F32)
            for d in (1, 2, 3):
                total += first_recv[d, dy].astype(F32)
            column_send[dy] = total.astype(BF16)
        for dy in (1, 3, 2):
            send(column_send.at[dy], column_recv.at[dy], vs.at[0], vr.at[0], (cent_at(4 - dy, 0), p))

        @pl.when(odd == 0)
        def _():
            arrived(second_recv.at[pl.ds(1, 3)], wr.at[1])
            for dy in range(4):
                total = second_send[0, dy].astype(F32)
                for d in (1, 2, 3):
                    total += second_recv[d, dy].astype(F32)
                late_send[dy] = total.astype(BF16)
            for dy in (1, 3, 2):
                send(late_send.at[dy], late_recv.at[dy], vs.at[1], vr.at[1], (cent_at(4 - dy, 0), p))

    def decode(parts, at):
        rows = sum(parts[1:], parts[0])
        token = jnp.minimum(lax.broadcasted_iota(jnp.int32, (32, DIM), 0), PLEN - 1)
        shift = 2 * jnp.where(token >= 15, token - 15, token)
        words = codes[at]
        word = jnp.where(token >= 15, words[1:2, :], words[0:1, :])
        level = jnp.right_shift(word, shift) & 3
        residual = jnp.where(
            level < 2,
            jnp.where(level == 0, book[0:1, :], book[1:2, :]),
            jnp.where(level == 2, book[2:3, :], book[3:4, :]),
        )
        vector = rows + residual
        squares = jnp.sum(vector * vector, axis=-1, keepdims=True)
        return (vector * lax.rsqrt(squares + 1e-06)).astype(BF16)

    def build_passages():
        arrived(column_recv.at[pl.ds(1, 3)], vr.at[0])
        built = decode([column_send[0].astype(F32)] + [column_recv[d].astype(F32) for d in (1, 2, 3)], c)

        @pl.when(odd == 0)
        def _():
            arrived(late_recv.at[pl.ds(1, 3)], vr.at[1])
            passages[pl.ds(0, 32), :] = built
            passages[pl.ds(32, 32), :] = decode(
                [late_send[0].astype(F32)] + [late_recv[d].astype(F32) for d in (1, 2, 3)], second_of
            )
            for d in (4, 3, 5, 2, 6, 1, 7):
                send(passages.at[pl.ds(0, 64)], passages.at[pl.ds(d * 64, 64)], us.at[0], ur.at[0], (c, pass_at(d)))

        @pl.when(odd == 1)
        def _():
            passages[pl.ds(EVEN, 32), :] = built
            for d in (4, 3, 5, 2, 6, 1, 7):
                send(
                    passages.at[pl.ds(EVEN, 32)], passages.at[pl.ds(EVEN + d * 32, 32)], us.at[0], ur.at[0], (c, pass_at(d))
                )

    def relay_passages():
        @pl.when(odd == 0)
        def _():
            arrived(passages.at[pl.ds(64, EVEN - 64)], ur.at[0])
            send(passages.at[pl.ds(0, EVEN)], passages.at[pl.ds(0, EVEN)], us.at[1], ur.at[1], (c, other))

        @pl.when(odd == 1)
        def _():
            arrived(passages.at[pl.ds(EVEN + 32, 224)], ur.at[0])
            send(passages.at[pl.ds(EVEN, 256)], passages.at[pl.ds(EVEN, 256)], us.at[1], ur.at[1], (c, other))

    def products():
        @pl.when(odd == 0)
        def _():
            arrived(passages.at[pl.ds(EVEN, 256)], ur.at[1])

        @pl.when(odd == 1)
        def _():
            arrived(passages.at[pl.ds(0, EVEN)], ur.at[1])

        lane = lax.broadcasted_iota(jnp.int32, (TOK, 128), 1)
        token = lax.broadcasted_iota(jnp.int32, (TOK, 128), 0)
        weights = jnp.where(lane >> 5 == token >> 5, 1.0 / QT, 0.0).astype(BF16)
        diagonal = ((lane & 31) == (token & 31))[:32]

        def one_tile(t, carry):
            tile = queries[pl.ds(pl.multiple_of(t * TILE, TILE), TILE), :]
            dots = lax.dot_general(passages[...], tile, (((1,), (1,)), ((), ())), preferred_element_type=F32)
            most = jnp.max(dots.reshape(24, 32, TILE), axis=1)
            for i in range(TILE // TOK):
                part = jnp.concatenate([most[:, i * TOK : (i + 1) * TOK], jnp.zeros((8, TOK), F32)], axis=0)
                high = part.astype(BF16)
                low = (part - high.astype(F32)).astype(BF16)
                means = jnp.dot(high, weights, preferred_element_type=F32) + jnp.dot(
                    low, weights, preferred_element_type=F32
                )
                row = jnp.sum(jnp.where(diagonal, means, 0.0), axis=0, keepdims=True)
                result_send[t * (TILE // TOK) + i, pl.ds(5, 1), :] = row
            return carry

        lax.fori_loop(0, NC * TOK // TILE, one_tile, 0)

    def send_result(d):
        target = (cent_at(4 - d // 4, 4 - d % 4), p)
        send(result_send.at[d], result_recv.at[d], us.at[2], ur.at[2], target)

    def step(s, carry):
        t, i = lax.div(s, STEPS), lax.rem(s, STEPS)

        @pl.when(s == 2)
        def _():
            sum_rows()

        @pl.when(s == 4)
        def _():
            arrived(queries.at[pl.ds(TILE, TILE)], qr.at[1])

        @pl.when(s == 5)
        def _():
            build_passages()

        @pl.when(s == 8)
        def _():
            arrived(queries.at[pl.ds(2 * TILE, TILE)], qr.at[2])

        @pl.when(s == 10)
        def _():
            relay_passages()

        @pl.when(s == 12)
        def _():
            arrived(queries.at[pl.ds(3 * TILE, TILE)], qr.at[3])
            products()
            for d in range(1, 12):
                send_result(d)

        tile = queries[pl.ds(pl.multiple_of(t * TILE, TILE), TILE), :]
        rows = cent[pl.ds(i * (CHUNK // 16), CHUNK // 16)].reshape(CHUNK, DIM)
        dots = lax.dot_general(rows, tile, (((1,), (1,)), ((), ())), preferred_element_type=F32)
        most = jnp.max(dots.reshape(CHUNK // 8, 8, TILE), axis=0)
        most = jnp.maximum(most, jnp.where(i == 0, -jnp.inf, running[...]))
        running[...] = most

        @pl.when(i == STEPS - 1)
        def _():
            best = jnp.max(most, axis=0, keepdims=True)
            held = probed[pl.ds(pl.multiple_of(t * 64, 64), 64), :]
            found = lax.dot_general(held, tile, (((1,), (1,)), ((), ())), preferred_element_type=F32)
            for j in range(TILE // TOK):
                block = found[j * 16 : (j + 1) * 16, j * TOK : (j + 1) * TOK]
                pair = jnp.where(group8 == sub8 >> 2, block[:8], 0.0) + jnp.where(
                    group8 - 2 == sub8 >> 2, block[8:], 0.0
                )
                four = pair + pltpu.roll(pair, 4, 0)
                result_send[t * (TILE // TOK) + j, pl.ds(0, 5), :] = jnp.where(
                    sub8 < 4, four, jnp.broadcast_to(best[:, j * TOK : (j + 1) * TOK], (8, 128))
                )[:5]

        return carry

    running[...] = jnp.full((8, TILE), -jnp.inf, F32)
    lax.fori_loop(0, NC * TOK // TILE * STEPS, step, 0)
    for d in range(12, NC):
        send_result(d)

    place = lane8 & 31
    even = place < 16
    away = jnp.where(even, place >> 1, place - 16)
    base = lax.rem(z + 16 - away, 8) * (2 * P_OWN)
    base = jnp.where(place < 24, base, -1000)
    second = even & ((place & 1) == 1)
    nothing = [jnp.zeros((8, 128), F32) for _ in range(CMAX // 8)]

    def combine(cc, got, best, total, chosen):
        late = lax.rem(cc, 2)
        at = base + P_OWN * jnp.where(even, late, 1 - late) + jnp.where(second, P_OWN - 8 + lax.div(cc, 2), cc)
        scores = jnp.broadcast_to(got[5:6, :], (8, 128))
        chosen = [
            jnp.where(wanted[pl.ds(8 * g, 8), :] == at, scores, chosen[g]) for g in range(CMAX // 8)
        ]
        return jnp.maximum(best, got), total + got, chosen

    held = combine(c, result_send[0], jnp.full((8, 128), -jnp.inf, F32), jnp.zeros((8, 128), F32), nothing)
    gone(queries.at[pl.ds(0, 3 * TOK)], qs.at[0])
    for d in (1, 2, 3):
        gone(queries.at[pl.ds(0, TILE)], qs.at[d])
    gone(first_send.at[pl.ds(1, 3)], ws.at[0])
    gone(column_send.at[pl.ds(1, 3)], vs.at[0])

    @pl.when(odd == 0)
    def _():
        gone(second_send.at[1], ws.at[1])
        gone(late_send.at[pl.ds(1, 3)], vs.at[1])
        gone(passages.at[pl.ds(0, 7 * 64)], us.at[0])
        gone(passages.at[pl.ds(0, EVEN)], us.at[1])

    @pl.when(odd == 1)
    def _():
        gone(second_send, ws.at[1])
        gone(passages.at[pl.ds(EVEN, 7 * 32)], us.at[0])
        gone(passages.at[pl.ds(EVEN, 256)], us.at[1])

    gone(result_send.at[pl.ds(1, NC - 1)], us.at[2])
    arrived(result_recv.at[pl.ds(1, NC - 1)], ur.at[2])
    for d in range(1, NC):
        held = combine(cent_at(d // 4, d % 4), result_recv[d], *held)
    best, total, chosen = held
    chosen = jnp.concatenate(chosen, axis=0)
    ones = jnp.where(group8 == sub8, 1.0, 0.0).astype(BF16)
    scores = jnp.zeros((8, CMAX), F32)
    for _ in range(3):
        term = chosen.astype(BF16)
        scores += lax.dot_general(ones, term, (((1,), (1,)), ((), ())), preferred_element_type=F32)
        chosen = chosen - term.astype(F32)
    score_out[...] = scores[:QD]
    for q in range(QD):
        top_out[pl.ds(q, 1), :] = best[4:5, q * QT : (q + 1) * QT]
        probe_out[q] = total[:4, q * QT : (q + 1) * QT]


def deliver(top, probe, score, top_out, probe_out, score_out, sems):
    copies = [
        pltpu.make_async_copy(src, dst, sems.at[i])
        for i, (src, dst) in enumerate(((top, top_out), (probe, probe_out), (score, score_out)))
    ]
    for copy in copies:
        copy.start()
    for copy in copies:
        copy.wait()


def body(queries, probes, centroids, codebook, token_cells, codes, locations, candidates, lengths):
    vmem = pl.BlockSpec(memory_space=pltpu.VMEM)
    hbm = pl.BlockSpec(memory_space=pltpu.HBM)
    results = pl.pallas_call(
        kernel,
        out_shape=(
            jax.ShapeDtypeStruct((QD, QT), F32),
            jax.ShapeDtypeStruct((QD, NPROBE, QT), F32),
            jax.ShapeDtypeStruct((QD, CMAX), F32),
        ),
        in_specs=[hbm] * 9,
        out_specs=(vmem, vmem, vmem),
        scratch_shapes=[
            pltpu.SMEM((NPROBE, NC * NP * QD), jnp.int32),
            pltpu.SMEM((P_OWN, PLEN), jnp.int32),
            pltpu.VMEM((P_OWN, 2, DIM), jnp.int32),
            pltpu.VMEM((4, DIM), F32),
            pltpu.SMEM((NP * P_OWN,), jnp.int32),
            pltpu.SMEM((QD, CMAX), jnp.int32),
            pltpu.SMEM((QD,), jnp.int32),
            pltpu.VMEM((SHARD // 16, 16, DIM), BF16),
            pltpu.VMEM((NC * TOK, DIM), BF16),
            pltpu.VMEM((4, 4, 32, DIM), BF16),
            pltpu.VMEM((4, 4, 32, DIM), BF16),
            pltpu.VMEM((2, 4, 32, DIM), BF16),
            pltpu.VMEM((4, 4, 32, DIM), BF16),
            pltpu.VMEM((4, 32, DIM), BF16),
            pltpu.VMEM((4, 32, DIM), BF16),
            pltpu.VMEM((4, 32, DIM), BF16),
            pltpu.VMEM((4, 32, DIM), BF16),
            pltpu.VMEM((NC * 16, DIM), BF16),
            pltpu.VMEM((EVEN + 256, DIM), BF16),
            pltpu.VMEM((NC, 8, 128), F32),
            pltpu.VMEM((NC, 8, 128), F32),
            pltpu.VMEM((CMAX, 128), jnp.int32),
            pltpu.VMEM((8, TILE), F32),
            pltpu.SemaphoreType.DMA((STEPS,)),
            pltpu.SemaphoreType.DMA((8,)),
        ]
        + [pltpu.SemaphoreType.DMA((4,))] * 8,
        compiler_params=pltpu.CompilerParams(
            collective_id=0, has_side_effects=True, vmem_limit_bytes=60 << 20
        ),
        name="late_interaction",
    )(
        queries.reshape(TOK, DIM), probes.T, token_cells, codes, codebook, locations, candidates, lengths,
        centroids.reshape(SHARD // 16, 16, DIM),
    )
    top, probe, score = pl.pallas_call(
        deliver,
        out_shape=tuple(jax.ShapeDtypeStruct(r.shape, r.dtype) for r in results),
        in_specs=[hbm] * 3,
        out_specs=[hbm] * 3,
        scratch_shapes=[pltpu.SemaphoreType.DMA((3,))],
        name="deliver",
    )(*results)
    return top, jnp.transpose(probe, (0, 2, 1)), score


def solution(mesh):
    placed = (
        P(("cent", "pass"), None, None),
        P(),
        P("cent", None),
        P(),
        P("pass", None),
        P("pass", None, None),
        P(),
        P(("cent", "pass"), None),
        P(("cent", "pass")),
    )
    return jax.shard_map(
        body,
        mesh=mesh,
        in_specs=placed,
        out_specs=(
            P(("cent", "pass"), None),
            P(("cent", "pass"), None, None),
            P(("cent", "pass"), None),
        ),
        check_vma=False,
    )
```

time: 48.4 us -> 46.3 us (0.957); the launches traced: 48.2 us -> 45.4 us
  Pallas kernels: 47.6 us -> 44.8 us
    pallas_call x1, Pallas kernels: 46.3 us -> 43.3 us  [body(): pl.pallas_call(kernel, out_shape=(jax.ShapeDtypeStruct((QD, QT), F32), ja...]
where the time goes in v3:
time: 46.3 us; the launch traced here: 45.4 us
  Pallas kernels  44.8 us (97%)
  between operations  0.64 us (1%)
    pallas_call x1, Pallas kernels, body(): pl.pallas_call(kernel, out_shape=(jax.ShapeDtypeStruct((QD, QT), F32), ja...  43.3 us
    pallas_call x1, Pallas kernels, body(): pl.pallas_call(deliver, out_shape=tuple((jax.ShapeDtypeStruct(r.shape, r....  1.5 us

profile of v3, /device:TPU:1, one launch (start us, length us, event | category | flops | bytes accessed | tf_op | source)
XLA Modules:
  0.0 45.4 jit_solution(10609733237541706853)
XLA Ops:
  0.6 43.3 %late_interaction.1 = (f32[4,32]{1,0:T(4,128)}, f32[4,4,32]{2,1,0:T(4,128)}, f32[4,40]{1,0:T(4,128)}) custom-call(bf16[128,128]{1,0:T(8,128)(2,1)} %bitcast.5, s32[4,1024]{1,0:T(4,128)} %bitcast.6, s32[24,30]{1,0:T(8,128)} %cells_hbm.1, s32[24,2,128]{2,1,0:T(2,128)} %codes_hbm.1, f32[4,128]{1,0:T(4,128)} %book_hbm.1, s32[384]{0:T(512)} %locations_hbm.1, ...), custom_call_target="tpu_custom_call" | custom-call | tf_op jit(solution)/shard_map/late_interaction/pallas_call | solution.py:412
  43.9 1.5 %deliver.1 = (f32[4,32]{1,0:T(4,128)}, f32[4,4,32]{2,1,0:T(4,128)}, f32[4,40]{1,0:T(4,128)}) custom-call(f32[4,32]{1,0:T(4,128)} %get-tuple-element.9.top, f32[4,4,32]{2,1,0:T(4,128)} %get-tuple-element.10.probe, f32[4,40]{1,0:T(4,128)} %get-tuple-element.11.score), custom_call_target="tpu_custom_call" | custom-call | tf_op jit(solution)/shard_map/deliver/pallas_call | solution.py:457

commit v4 on v3

--- a/solution.py
+++ b/solution.py
@@ -32,7 +32,7 @@
     probes, cells, codes, book, locations, candidates, lengths,
     cent, queries, first_send, first_recv, second_send, second_recv, column_send, column_recv, late_send, late_recv,
     probed, passages, result_send, result_recv, wanted, running,
-    load_sem, small_sem, qs, qr, ws, wr, vs, vr, us, ur,
+    load_sem, small_sem, plane_here, line_here, qs, qr, ws, wr, vs, vr, us, ur,
 ):
     c = lax.axis_index("cent")
     p = lax.axis_index("pass")
@@ -74,15 +74,24 @@
         load.start()
 
     barrier = pltpu.get_barrier_semaphore()
-    partners = (
-        [(cent_at(0, d), p) for d in (1, 2, 3)]
-        + [(cent_at(d, 0), p) for d in (1, 2, 3)]
-        + [(c, pass_at(d)) for d in range(1, 8)]
-        + [(c, other)]
-    )
-    for partner in partners:
-        pl.semaphore_signal(barrier, inc=1, device_id=partner, device_id_type=MESH)
-    pl.semaphore_wait(barrier, len(partners))
+    for d in (1, 2, 3):
+        for there in (cent_at(0, d), cent_at(d, 0)):
+            pl.semaphore_signal(barrier, inc=1, device_id=(there, z * 2), device_id_type=MESH)
+    for d in range(1, 8):
+        pl.semaphore_signal(
+            barrier, inc=1, device_id=(c, lax.rem(z + d, 8) * 2 + 1), device_id_type=MESH
+        )
+
+    @pl.when(core == 1)
+    def _():
+        pl.semaphore_signal(barrier, inc=1, device_id=(c, other), device_id_type=MESH)
+        pl.semaphore_wait(plane_here, 1)
+
+    @pl.when(core == 0)
+    def _():
+        pl.semaphore_wait(barrier, 13)
+        pl.semaphore_signal(plane_here, inc=1, device_id=(c, other), device_id_type=MESH)
+
     for load in small:
         load.wait()
     lane8 = lax.broadcasted_iota(jnp.int32, (8, 128), 1)
@@ -213,6 +222,16 @@
         squares = jnp.sum(vector * vector, axis=-1, keepdims=True)
         return (vector * lax.rsqrt(squares + 1e-06)).astype(BF16)
 
+    def await_line():
+        @pl.when(core == 1)
+        def _():
+            pl.semaphore_wait(barrier, 14)
+            pl.semaphore_signal(line_here, inc=1, device_id=(c, other), device_id_type=MESH)
+
+        @pl.when(core == 0)
+        def _():
+            pl.semaphore_wait(line_here, 1)
+
     def build_passages():
         arrived(column_recv.at[pl.ds(1, 3)], vr.at[0])
         built = decode([column_send[0].astype(F32)] + [column_recv[d].astype(F32) for d in (1, 2, 3)], c)
@@ -294,19 +313,23 @@
 
         @pl.when(s == 5)
         def _():
+            await_line()
             build_passages()
 
         @pl.when(s == 8)
         def _():
             arrived(queries.at[pl.ds(2 * TILE, TILE)], qr.at[2])
 
-        @pl.when(s == 10)
+        @pl.when(s == 13)
         def _():
             relay_passages()
 
         @pl.when(s == 12)
         def _():
             arrived(queries.at[pl.ds(3 * TILE, TILE)], qr.at[3])
+
+        @pl.when(s == 15)
+        def _():
             products()
             for d in range(1, 12):
                 send_result(d)
@@ -444,6 +467,8 @@
             pltpu.VMEM((8, TILE), F32),
             pltpu.SemaphoreType.DMA((STEPS,)),
             pltpu.SemaphoreType.DMA((8,)),
+            pltpu.SemaphoreType.REGULAR,
+            pltpu.SemaphoreType.REGULAR,
         ]
         + [pltpu.SemaphoreType.DMA((4,))] * 8,
         compiler_params=pltpu.CompilerParams(

time: 46.3 us -> 42.1 us (0.909); the launches traced: 45.4 us -> 42 us
  Pallas kernels: 44.8 us -> 41.4 us
    pallas_call x1, Pallas kernels: 43.3 us -> 39.9 us  [body(): pl.pallas_call(kernel, out_shape=(jax.ShapeDtypeStruct((QD, QT), F32), ja...]
where the time goes in v4:
time: 42.1 us; the launch traced here: 42 us
  Pallas kernels  41.4 us (98%)
  between operations  0.64 us (2%)
    pallas_call x1, Pallas kernels, body(): pl.pallas_call(kernel, out_shape=(jax.ShapeDtypeStruct((QD, QT), F32), ja...  39.9 us
    pallas_call x1, Pallas kernels, body(): pl.pallas_call(deliver, out_shape=tuple((jax.ShapeDtypeStruct(r.shape, r....  1.5 us

profile of v4, /device:TPU:1, one launch (start us, length us, event | category | flops | bytes accessed | tf_op | source)
XLA Modules:
  0.0 42.0 jit_solution(6282938497161680660)
XLA Ops:
  0.6 39.9 %late_interaction.1 = (f32[4,32]{1,0:T(4,128)}, f32[4,4,32]{2,1,0:T(4,128)}, f32[4,40]{1,0:T(4,128)}) custom-call(bf16[128,128]{1,0:T(8,128)(2,1)} %bitcast.5, s32[4,1024]{1,0:T(4,128)} %bitcast.6, s32[24,30]{1,0:T(8,128)} %cells_hbm.1, s32[24,2,128]{2,1,0:T(2,128)} %codes_hbm.1, f32[4,128]{1,0:T(4,128)} %book_hbm.1, s32[384]{0:T(512)} %locations_hbm.1, ...), custom_call_target="tpu_custom_call" | custom-call | tf_op jit(solution)/shard_map/late_interaction/pallas_call | solution.py:435
  40.5 1.5 %deliver.1 = (f32[4,32]{1,0:T(4,128)}, f32[4,4,32]{2,1,0:T(4,128)}, f32[4,40]{1,0:T(4,128)}) custom-call(f32[4,32]{1,0:T(4,128)} %get-tuple-element.9.top, f32[4,4,32]{2,1,0:T(4,128)} %get-tuple-element.10.probe, f32[4,40]{1,0:T(4,128)} %get-tuple-element.11.score), custom_call_target="tpu_custom_call" | custom-call | tf_op jit(solution)/shard_map/deliver/pallas_call | solution.py:482

commit v5 on v4

--- a/solution.py
+++ b/solution.py
@@ -20,7 +20,11 @@
 SHIFT = 14
 CHUNK = 4096
 TILE = 512
+WIDE = 1024
 STEPS = SHARD // CHUNK
+SUM_AT = 3
+BUILD_AT = 6
+PRODUCTS_AT = 14
 EVEN = 8 * 64
 F32 = jnp.float32
 BF16 = jnp.bfloat16
@@ -28,7 +32,7 @@
 
 def kernel(
     q_hbm, probes_hbm, cells_hbm, codes_hbm, book_hbm, locations_hbm, candidates_hbm, lengths_hbm, cent_hbm,
-    top_out, probe_out, score_out,
+    out,
     probes, cells, codes, book, locations, candidates, lengths,
     cent, queries, first_send, first_recv, second_send, second_recv, column_send, column_recv, late_send, late_recv,
     probed, passages, result_send, result_recv, wanted, running,
@@ -74,7 +78,7 @@
         load.start()
 
     barrier = pltpu.get_barrier_semaphore()
-    for d in (1, 2, 3):
+    for d in (2, 1, 3):
         for there in (cent_at(0, d), cent_at(d, 0)):
             pl.semaphore_signal(barrier, inc=1, device_id=(there, z * 2), device_id_type=MESH)
     for d in range(1, 8):
@@ -92,8 +96,7 @@
         pl.semaphore_wait(barrier, 13)
         pl.semaphore_signal(plane_here, inc=1, device_id=(c, other), device_id_type=MESH)
 
-    for load in small:
-        load.wait()
+    small[0].wait()
     lane8 = lax.broadcasted_iota(jnp.int32, (8, 128), 1)
     sub8 = lax.broadcasted_iota(jnp.int32, (8, 128), 0)
 
@@ -114,7 +117,7 @@
 
     for d in (1, 3, 2):
         send(queries.at[pl.ds(0, TOK)], queries.at[pl.ds(d * TOK, TOK)], qs.at[0], qr.at[0], (cent_at(0, d), p))
-    for load in loads:
+    for load in small[1:] + loads:
         load.wait()
 
     mine = [jnp.where(sub8 == r, c, -1) for r in range(8)]
@@ -144,12 +147,11 @@
         second_send[half, dy] = pick([cells[at, min(j, PLEN - 1)] for j in range(32)])
         return carry
 
-    def collect_probed(d, carry):
+    def collect_probed(d):
         base = (cent_at(4 - lax.div(d, 4), 4 - lax.rem(d, 4)) * NP + p) * QD
         probed[pl.ds(pl.multiple_of(d * 16, 16), 16), :] = pick(
             [probes[k, base + q] for q in range(QD) for k in range(NPROBE)]
         )
-        return carry
 
     lax.fori_loop(0, 12, collect_first, 0)
     for d in (1, 3, 2):
@@ -171,8 +173,6 @@
     arrived(queries.at[pl.ds(TOK, 3 * TOK)], qr.at[0])
     for d in (1, 3, 2):
         send(queries.at[pl.ds(0, TILE)], queries.at[pl.ds(d * TILE, TILE)], qs.at[d], qr.at[d], (cent_at(d, 0), p))
-    lax.fori_loop(12, 16, collect_first, 0)
-    lax.fori_loop(0, NC, collect_probed, 0)
 
     group8 = lane8 >> 5
     for base in range(0, CMAX, 8):
@@ -232,6 +232,13 @@
         def _():
             pl.semaphore_wait(line_here, 1)
 
+    def send_passages(start, size, d, near):
+        i = 0 if near else 1
+        there = pass_at(d) if near else lax.rem(z + d, 8) * 2 + 1 - core
+        send(
+            passages.at[pl.ds(start, size)], passages.at[pl.ds(start + d * size, size)], us.at[i], ur.at[i], (c, there)
+        )
+
     def build_passages():
         arrived(column_recv.at[pl.ds(1, 3)], vr.at[0])
         built = decode([column_send[0].astype(F32)] + [column_recv[d].astype(F32) for d in (1, 2, 3)], c)
@@ -243,35 +250,26 @@
             passages[pl.ds(32, 32), :] = decode(
                 [late_send[0].astype(F32)] + [late_recv[d].astype(F32) for d in (1, 2, 3)], second_of
             )
-            for d in (4, 3, 5, 2, 6, 1, 7):
-                send(passages.at[pl.ds(0, 64)], passages.at[pl.ds(d * 64, 64)], us.at[0], ur.at[0], (c, pass_at(d)))
+            for d in (4, 3, 5, 2, 6, 1, 7, 0):
+                for near in ((True, False) if d else (False,)):
+                    send_passages(0, 64, d, near)
 
         @pl.when(odd == 1)
         def _():
             passages[pl.ds(EVEN, 32), :] = built
-            for d in (4, 3, 5, 2, 6, 1, 7):
-                send(
-                    passages.at[pl.ds(EVEN, 32)], passages.at[pl.ds(EVEN + d * 32, 32)], us.at[0], ur.at[0], (c, pass_at(d))
-                )
-
-    def relay_passages():
-        @pl.when(odd == 0)
-        def _():
-            arrived(passages.at[pl.ds(64, EVEN - 64)], ur.at[0])
-            send(passages.at[pl.ds(0, EVEN)], passages.at[pl.ds(0, EVEN)], us.at[1], ur.at[1], (c, other))
-
-        @pl.when(odd == 1)
-        def _():
-            arrived(passages.at[pl.ds(EVEN + 32, 224)], ur.at[0])
-            send(passages.at[pl.ds(EVEN, 256)], passages.at[pl.ds(EVEN, 256)], us.at[1], ur.at[1], (c, other))
+            for d in (4, 3, 5, 2, 6, 1, 7, 0):
+                for near in ((True, False) if d else (False,)):
+                    send_passages(EVEN, 32, d, near)
 
     def products():
         @pl.when(odd == 0)
         def _():
+            arrived(passages.at[pl.ds(64, EVEN - 64)], ur.at[0])
             arrived(passages.at[pl.ds(EVEN, 256)], ur.at[1])
 
         @pl.when(odd == 1)
         def _():
+            arrived(passages.at[pl.ds(EVEN + 32, 224)], ur.at[0])
             arrived(passages.at[pl.ds(0, EVEN)], ur.at[1])
 
         lane = lax.broadcasted_iota(jnp.int32, (TOK, 128), 1)
@@ -280,10 +278,10 @@
         diagonal = ((lane & 31) == (token & 31))[:32]
 
         def one_tile(t, carry):
-            tile = queries[pl.ds(pl.multiple_of(t * TILE, TILE), TILE), :]
+            tile = queries[pl.ds(pl.multiple_of(t * WIDE, WIDE), WIDE), :]
             dots = lax.dot_general(passages[...], tile, (((1,), (1,)), ((), ())), preferred_element_type=F32)
-            most = jnp.max(dots.reshape(24, 32, TILE), axis=1)
-            for i in range(TILE // TOK):
+            most = jnp.max(dots.reshape(24, 32, WIDE), axis=1)
+            for i in range(WIDE // TOK):
                 part = jnp.concatenate([most[:, i * TOK : (i + 1) * TOK], jnp.zeros((8, TOK), F32)], axis=0)
                 high = part.astype(BF16)
                 low = (part - high.astype(F32)).astype(BF16)
@@ -291,76 +289,91 @@
                     low, weights, preferred_element_type=F32
                 )
                 row = jnp.sum(jnp.where(diagonal, means, 0.0), axis=0, keepdims=True)
-                result_send[t * (TILE // TOK) + i, pl.ds(5, 1), :] = row
+                result_send[t * (WIDE // TOK) + i, pl.ds(5, 1), :] = row
             return carry
 
-        lax.fori_loop(0, NC * TOK // TILE, one_tile, 0)
+        lax.fori_loop(0, NC * TOK // WIDE, one_tile, 0)
 
     def send_result(d):
         target = (cent_at(4 - d // 4, 4 - d % 4), p)
         send(result_send.at[d], result_recv.at[d], us.at[2], ur.at[2], target)
 
-    def step(s, carry):
+    def tile_of(t):
+        return queries[pl.ds(pl.multiple_of(t * TILE, TILE), TILE), :]
+
+    def scan(t, start, size, fresh):
+        rows = cent[pl.ds(start * (CHUNK // 16), size // 16)].reshape(size, DIM)
+        dots = lax.dot_general(rows, tile_of(t), (((1,), (1,)), ((), ())), preferred_element_type=F32)
+        most = jnp.max(dots.reshape(size // 8, 8, TILE), axis=0)
+        running[...] = jnp.maximum(most, jnp.where(fresh, -jnp.inf, running[...]))
+
+    def close_tile(t):
+        best = jnp.max(running[...], axis=0, keepdims=True)
+        held = probed[pl.ds(pl.multiple_of(t * 64, 64), 64), :]
+        found = lax.dot_general(held, tile_of(t), (((1,), (1,)), ((), ())), preferred_element_type=F32)
+        for j in range(TILE // TOK):
+            block = found[j * 16 : (j + 1) * 16, j * TOK : (j + 1) * TOK]
+            pair = jnp.where(group8 == sub8 >> 2, block[:8], 0.0) + jnp.where(
+                group8 - 2 == sub8 >> 2, block[8:], 0.0
+            )
+            four = pair + pltpu.roll(pair, 4, 0)
+            result_send[t * (TILE // TOK) + j, pl.ds(0, 5), :] = jnp.where(
+                sub8 < 4, four, jnp.broadcast_to(best[:, j * TOK : (j + 1) * TOK], (8, 128))
+            )[:5]
+
+    def first_step(i, carry):
+        @pl.when(i == SUM_AT)
+        def _():
+            sum_rows()
+
+        scan(0, i, CHUNK, i == 0)
+        for k in range(4):
+            collect_probed(4 * i + k)
+        for k in range(2):
+            collect_first(12 + 2 * lax.rem(i, 2) + k, 0)
+        return carry
+
+    running[...] = jnp.full((8, TILE), -jnp.inf, F32)
+    lax.fori_loop(0, STEPS, first_step, 0)
+    close_tile(0)
+
+    def step(n, carry):
+        s = 2 * n
         t, i = lax.div(s, STEPS), lax.rem(s, STEPS)
 
-        @pl.when(s == 2)
-        def _():
-            sum_rows()
-
-        @pl.when(s == 4)
+        @pl.when(s == STEPS)
         def _():
             arrived(queries.at[pl.ds(TILE, TILE)], qr.at[1])
 
-        @pl.when(s == 5)
+        @pl.when(s == BUILD_AT)
         def _():
             await_line()
             build_passages()
 
-        @pl.when(s == 8)
+        @pl.when(s == 2 * STEPS)
         def _():
             arrived(queries.at[pl.ds(2 * TILE, TILE)], qr.at[2])
 
-        @pl.when(s == 13)
-        def _():
-            relay_passages()
-
-        @pl.when(s == 12)
+        @pl.when(s == 3 * STEPS)
         def _():
             arrived(queries.at[pl.ds(3 * TILE, TILE)], qr.at[3])
 
-        @pl.when(s == 15)
+        @pl.when(s == PRODUCTS_AT)
         def _():
             products()
-            for d in range(1, 12):
+            for d in (10, 9, 11, 6, 2, 5, 7, 8, 1, 3, 4):
                 send_result(d)
 
-        tile = queries[pl.ds(pl.multiple_of(t * TILE, TILE), TILE), :]
-        rows = cent[pl.ds(i * (CHUNK // 16), CHUNK // 16)].reshape(CHUNK, DIM)
-        dots = lax.dot_general(rows, tile, (((1,), (1,)), ((), ())), preferred_element_type=F32)
-        most = jnp.max(dots.reshape(CHUNK // 8, 8, TILE), axis=0)
-        most = jnp.maximum(most, jnp.where(i == 0, -jnp.inf, running[...]))
-        running[...] = most
-
-        @pl.when(i == STEPS - 1)
-        def _():
-            best = jnp.max(most, axis=0, keepdims=True)
-            held = probed[pl.ds(pl.multiple_of(t * 64, 64), 64), :]
-            found = lax.dot_general(held, tile, (((1,), (1,)), ((), ())), preferred_element_type=F32)
-            for j in range(TILE // TOK):
-                block = found[j * 16 : (j + 1) * 16, j * TOK : (j + 1) * TOK]
-                pair = jnp.where(group8 == sub8 >> 2, block[:8], 0.0) + jnp.where(
-                    group8 - 2 == sub8 >> 2, block[8:], 0.0
-                )
-                four = pair + pltpu.roll(pair, 4, 0)
-                result_send[t * (TILE // TOK) + j, pl.ds(0, 5), :] = jnp.where(
-                    sub8 < 4, four, jnp.broadcast_to(best[:, j * TOK : (j + 1) * TOK], (8, 128))
-                )[:5]
+        scan(t, i, 2 * CHUNK, i == 0)
+
+        @pl.when(i == STEPS - 2)
+        def _():
+            close_tile(t)
 
         return carry
 
-    running[...] = jnp.full((8, TILE), -jnp.inf, F32)
-    lax.fori_loop(0, NC * TOK // TILE * STEPS, step, 0)
-    for d in range(12, NC):
+    lax.fori_loop(STEPS // 2, NC * TOK // TILE * STEPS // 2, step, 0)
+    for d in (14, 13, 15, 12):
         send_result(d)
 
     place = lane8 & 31
@@ -412,21 +425,16 @@
         term = chosen.astype(BF16)
         scores += lax.dot_general(ones, term, (((1,), (1,)), ((), ())), preferred_element_type=F32)
         chosen = chosen - term.astype(F32)
-    score_out[...] = scores[:QD]
+    out[pl.ds(0, 8), :] = total
+    out[pl.ds(4, 1), :] = best[4:5]
+    out[pl.ds(8, 8), pl.ds(0, CMAX)] = scores
+
+
+def deliver(got, top_out, probe_out, score_out):
     for q in range(QD):
-        top_out[pl.ds(q, 1), :] = best[4:5, q * QT : (q + 1) * QT]
-        probe_out[q] = total[:4, q * QT : (q + 1) * QT]
-
-
-def deliver(top, probe, score, top_out, probe_out, score_out, sems):
-    copies = [
-        pltpu.make_async_copy(src, dst, sems.at[i])
-        for i, (src, dst) in enumerate(((top, top_out), (probe, probe_out), (score, score_out)))
-    ]
-    for copy in copies:
-        copy.start()
-    for copy in copies:
-        copy.wait()
+        top_out[pl.ds(q, 1), :] = got[4:5, q * QT : (q + 1) * QT]
+        probe_out[q] = got[:4, q * QT : (q + 1) * QT]
+    score_out[...] = got[8 : 8 + QD, :CMAX]
 
 
 def body(queries, probes, centroids, codebook, token_cells, codes, locations, candidates, lengths):
@@ -434,13 +442,9 @@
     hbm = pl.BlockSpec(memory_space=pltpu.HBM)
     results = pl.pallas_call(
         kernel,
-        out_shape=(
-            jax.ShapeDtypeStruct((QD, QT), F32),
-            jax.ShapeDtypeStruct((QD, NPROBE, QT), F32),
-            jax.ShapeDtypeStruct((QD, CMAX), F32),
-        ),
+        out_shape=jax.ShapeDtypeStruct((16, 128), F32),
         in_specs=[hbm] * 9,
-        out_specs=(vmem, vmem, vmem),
+        out_specs=vmem,
         scratch_shapes=[
             pltpu.SMEM((NPROBE, NC * NP * QD), jnp.int32),
             pltpu.SMEM((P_OWN, PLEN), jnp.int32),
@@ -481,12 +485,15 @@
     )
     top, probe, score = pl.pallas_call(
         deliver,
-        out_shape=tuple(jax.ShapeDtypeStruct(r.shape, r.dtype) for r in results),
-        in_specs=[hbm] * 3,
-        out_specs=[hbm] * 3,
-        scratch_shapes=[pltpu.SemaphoreType.DMA((3,))],
+        out_shape=(
+            jax.ShapeDtypeStruct((QD, QT), F32),
+            jax.ShapeDtypeStruct((QD, NPROBE, QT), F32),
+            jax.ShapeDtypeStruct((QD, CMAX), F32),
+        ),
+        in_specs=[vmem],
+        out_specs=[vmem] * 3,
         name="deliver",
-    )(*results)
+    )(results)
     return top, jnp.transpose(probe, (0, 2, 1)), score
 
 

time: 42.1 us -> 40.7 us (0.967)
  Pallas kernels: 41.4 us -> 39.9 us
    pallas_call x2, Pallas kernels: 41.4 us -> 39.9 us  [the longest x1 38.5 us: body(): pl.pallas_call(kernel, out_shape=jax.ShapeDtypeStruct((16, 128), F32), in...]
where the time goes in v5:
time: 40.7 us; the launch traced here: 40.6 us
  Pallas kernels  39.9 us (98%)
  between operations  0.64 us (2%)
    pallas_call x1, Pallas kernels, body(): pl.pallas_call(kernel, out_shape=jax.ShapeDtypeStruct((16, 128), F32), in...  38.5 us
    pallas_call x1, Pallas kernels, body(): pl.pallas_call(deliver, out_shape=(jax.ShapeDtypeStruct((QD, QT), F32), j...  1.37 us

profile of v5, /device:TPU:1, one launch (start us, length us, event | category | flops | bytes accessed | tf_op | source)
XLA Modules:
  0.0 40.6 jit_solution(4486123581618628697)
XLA Ops:
  0.6 38.5 %late_interaction.1.got = f32[16,128]{1,0:T(8,128)} custom-call(bf16[128,128]{1,0:T(8,128)(2,1)} %bitcast.5, s32[4,1024]{1,0:T(4,128)} %bitcast.6, s32[24,30]{1,0:T(8,128)} %cells_hbm.1, s32[24,2,128]{2,1,0:T(2,128)} %codes_hbm.1, f32[4,128]{1,0:T(4,128)} %book_hbm.1, s32[384]{0:T(512)} %locations_hbm.1, s32[4,40]{1,0:T(4,128)} %candidates_hbm.1, ...), custom_call_target="tpu_custom_call" | custom-call | tf_op jit(solution)/shard_map/late_interaction/pallas_call | solution.py:443
  39.2 1.4 %deliver.1 = (f32[4,32]{1,0:T(4,128)}, f32[4,4,32]{2,1,0:T(4,128)}, f32[4,40]{1,0:T(4,128)}) custom-call(f32[16,128]{1,0:T(8,128)} %late_interaction.1.got), custom_call_target="tpu_custom_call" | custom-call | tf_op jit(solution)/shard_map/deliver/pallas_call | solution.py:486

commit v6 on v5

--- a/solution.py
+++ b/solution.py
@@ -22,7 +22,7 @@
 TILE = 512
 WIDE = 1024
 STEPS = SHARD // CHUNK
-SUM_AT = 3
+SUM_AT = 2
 BUILD_AT = 6
 PRODUCTS_AT = 14
 EVEN = 8 * 64
@@ -322,19 +322,19 @@
             )[:5]
 
     def first_step(i, carry):
-        @pl.when(i == SUM_AT)
+        @pl.when(i == SUM_AT // 2)
         def _():
             sum_rows()
 
-        scan(0, i, CHUNK, i == 0)
+        scan(0, 2 * i, 2 * CHUNK, i == 0)
+        for k in range(8):
+            collect_probed(8 * i + k)
         for k in range(4):
-            collect_probed(4 * i + k)
-        for k in range(2):
-            collect_first(12 + 2 * lax.rem(i, 2) + k, 0)
+            collect_first(12 + k, 0)
         return carry
 
     running[...] = jnp.full((8, TILE), -jnp.inf, F32)
-    lax.fori_loop(0, STEPS, first_step, 0)
+    lax.fori_loop(0, STEPS // 2, first_step, 0)
     close_tile(0)
 
     def step(n, carry):

time: 40.7 us -> 40.5 us (level)
  no operation moved by 1% of the time
where the time goes in v6:
time: 40.5 us; the launch traced here: 40.4 us
  Pallas kernels  39.7 us (98%)
  between operations  0.64 us (2%)
    pallas_call x1, Pallas kernels, body(): pl.pallas_call(kernel, out_shape=jax.ShapeDtypeStruct((16, 128), F32), in...  38.4 us
    pallas_call x1, Pallas kernels, body(): pl.pallas_call(deliver, out_shape=(jax.ShapeDtypeStruct((QD, QT), F32), j...  1.37 us

profile of v6, /device:TPU:1, one launch (start us, length us, event | category | flops | bytes accessed | tf_op | source)
XLA Modules:
  0.0 40.4 jit_solution(1161923407317242868)
XLA Ops:
  0.6 38.4 %late_interaction.1.got = f32[16,128]{1,0:T(8,128)} custom-call(bf16[128,128]{1,0:T(8,128)(2,1)} %bitcast.5, s32[4,1024]{1,0:T(4,128)} %bitcast.6, s32[24,30]{1,0:T(8,128)} %cells_hbm.1, s32[24,2,128]{2,1,0:T(2,128)} %codes_hbm.1, f32[4,128]{1,0:T(4,128)} %book_hbm.1, s32[384]{0:T(512)} %locations_hbm.1, s32[4,40]{1,0:T(4,128)} %candidates_hbm.1, ...), custom_call_target="tpu_custom_call" | custom-call | tf_op jit(solution)/shard_map/late_interaction/pallas_call | solution.py:443
  39.0 1.4 %deliver.1 = (f32[4,32]{1,0:T(4,128)}, f32[4,4,32]{2,1,0:T(4,128)}, f32[4,40]{1,0:T(4,128)}) custom-call(f32[16,128]{1,0:T(8,128)} %late_interaction.1.got), custom_call_target="tpu_custom_call" | custom-call | tf_op jit(solution)/shard_map/deliver/pallas_call | solution.py:486
